TPU v7x, 512 devices: a whole 4x4x16 slice. The times are simulated.
512 devices in a mesh: dp: 4 (over y), ctx: 32 (over x, z_lo), tp: 4 (over z_hi, core).
Axes of the slice: x: 4, y: 4, z: 16 (z_hi: 2, z_lo: 8; z = z_hi * 8 + z_lo), core: 2. Of those that a mesh axis runs over, the one named last changes fastest.
Arguments:
- queries: bfloat16 [4, 4096, 4096], P('dp', 'ctx', 'tp'), may hold values from -6 to 6
- keys: bfloat16 [4, 4096, 512], P('dp', 'ctx', 'tp'), may hold values from -6 to 6
- values: bfloat16 [4, 4096, 512], P('dp', 'ctx', 'tp'), may hold values from -6 to 6
- out_grad: bfloat16 [4, 4096, 4096], P('dp', 'ctx', 'tp'), may hold values from -6 to 6
- mixed_grad: bfloat16 [16384, 2048], P(('dp', 'ctx'), 'tp'), may hold values from -6 to 6
- expert_ids: int32 [16384, 8], P(('dp', 'ctx')), may hold values from 0 to 127, all different within a row; in each aligned block of 128 rows (0 to 127, 128 to 255, ...) at most 10 rows name the same one
- combine: bfloat16 [16384, 8], P(('dp', 'ctx')), may hold values from 0.049804688 to 1
- w_down: bfloat16 [128, 1536, 2048], P(('dp', 'ctx'), 'tp'), may hold values from -0.125 to 0.125
Outputs:
- query_grad: bfloat16 [4, 4096, 4096], P('dp', 'ctx', 'tp')
- key_grad: bfloat16 [4, 4096, 512], P('dp', 'ctx', 'tp')
- value_grad: bfloat16 [4, 4096, 512], P('dp', 'ctx', 'tp')
- hidden_grad: bfloat16 [128, 128, 10, 1536], P(('dp', 'ctx'), None, None, 'tp')
Inputs may be any that keep to these rules, and one draw needn't show every extreme that they name: `expert_ids`: each row names 8 distinct experts. Within each aligned block of 128 rows no expert is named more than 10 times, a bound that some block reaches.
All inputs are finite; a program needn't handle non-finite values.
Results may differ from a plain program's by a relative error of at most 0.0071.
Values may be sent and summed in bfloat16 or wider, within the bound.
A program may use at most 128 MiB of HBM per device.

v0:
```python
import math

import jax
import jax.numpy as jnp
from jax import lax
from jax.sharding import PartitionSpec as P

HEADS = 32
KV_HEADS = 4
HEAD_DIM = 128
TOPK = 8


masked_score = -1e30


def make_set(query_rows, grad_rows, first_row, kv_local):
    row_count = query_rows.shape[0]
    positions = first_row + jnp.arange(row_count, dtype=jnp.int32)
    return (
        query_rows.reshape(row_count, kv_local, -1, HEAD_DIM),
        grad_rows.reshape(row_count, kv_local, -1, HEAD_DIM),
        positions,
    )


def key_blocks(piece):
    key_part, value_part = piece
    length = key_part.shape[0]
    block_size = math.gcd(length, 512)
    shape = (length // block_size, block_size) + key_part.shape[1:]
    return (key_part.reshape(shape), value_part.reshape(shape), block_size)


def block_scores(query_rows, positions, key_block, block_start, score_scale):
    scores = (
        jnp.einsum("rghd,sgd->ghrs", query_rows, key_block, preferred_element_type=jnp.float32)
        * score_scale
    )
    key_places = block_start + jnp.arange(key_block.shape[0], dtype=jnp.int32)
    allowed = key_places[None, :] <= positions[:, None]
    return (jnp.where(allowed, scores, masked_score), allowed)


def stats_update(state, query_set, key_block, value_block, block_start, score_scale):
    query_rows, grad_rows, positions = query_set

    def stats_compute(state):
        top, total, accum = state
        scores, allowed = block_scores(query_rows, positions, key_block, block_start, score_scale)
        new_top = jnp.maximum(top, jnp.max(scores, axis=-1))
        weights = jnp.where(allowed, jnp.exp(scores - new_top[..., None]), 0.0)
        grads = jnp.einsum(
            "rghd,sgd->ghrs", grad_rows, value_block, preferred_element_type=jnp.float32
        )
        shrink = jnp.exp(top - new_top)
        return (
            new_top,
            total * shrink + jnp.sum(weights, axis=-1),
            accum * shrink + jnp.sum(weights * grads, axis=-1),
        )

    return lax.cond(block_start <= positions[-1], stats_compute, lambda kept: kept, state)


def grads_update(
    state, query_set, stats, key_block, value_block, block_start, slot_start, score_scale
):
    query_rows, grad_rows, positions = query_set
    log_total, delta = stats

    def grads_compute(state):
        query_total, key_value_total = state
        scores, allowed = block_scores(query_rows, positions, key_block, block_start, score_scale)
        probs = jnp.where(allowed, jnp.exp(scores - log_total[..., None]), 0.0)
        grads = jnp.einsum(
            "rghd,sgd->ghrs", grad_rows, value_block, preferred_element_type=jnp.float32
        )
        dscore = probs * (grads - delta[..., None])
        probs_low = probs.astype(jnp.bfloat16)
        dscore_low = dscore.astype(jnp.bfloat16)
        query_total = query_total + jnp.einsum(
            "ghrs,sgd->rghd", dscore_low, key_block, preferred_element_type=jnp.float32
        )
        key_part = jnp.einsum(
            "ghrs,rghd->sgd", dscore_low, query_rows, preferred_element_type=jnp.float32
        )
        value_part = jnp.einsum(
            "ghrs,rghd->sgd", probs_low, grad_rows, preferred_element_type=jnp.float32
        )
        current = lax.dynamic_slice_in_dim(key_value_total, slot_start, key_block.shape[0], 0)
        key_value_total = lax.dynamic_update_slice_in_dim(
            key_value_total, current + jnp.stack([key_part, value_part], axis=1), slot_start, 0
        )
        return (query_total, key_value_total)

    return lax.cond(block_start <= positions[-1], grads_compute, lambda kept: kept, state)


def per_device(queries, keys, values, out_grad, mixed_grad, expert_ids, combine, w_down):
    score_scale = HEAD_DIM ** (-0.5)
    local_queries = queries[0]
    local_grads = out_grad[0]
    rows_dev = local_queries.shape[0]
    kv_local = keys.shape[2] // HEAD_DIM
    group = HEADS // KV_HEADS
    n_ctx = lax.axis_size("ctx")
    position = lax.axis_index("ctx")
    all_keys = rows_dev * n_ctx
    key_heads = keys[0].reshape(rows_dev, kv_local, HEAD_DIM)
    value_heads = values[0].reshape(rows_dev, kv_local, HEAD_DIM)
    query_sets = (make_set(local_queries, local_grads, position * rows_dev, kv_local),)
    stats_start = tuple(
        (
            (
                jnp.full((kv_local, group, query_set[2].shape[0]), masked_score, jnp.float32),
                jnp.zeros((kv_local, group, query_set[2].shape[0]), jnp.float32),
                jnp.zeros((kv_local, group, query_set[2].shape[0]), jnp.float32),
            )
            for query_set in query_sets
        )
    )
    carry = stats_start
    key_stack, value_stack, block_size = key_blocks(
        (
            lax.all_gather(key_heads, "ctx", axis=0, tiled=True),
            lax.all_gather(value_heads, "ctx", axis=0, tiled=True),
        )
    )

    def stats_one_block(index, carry):
        block_start = index * block_size
        return tuple(
            (
                stats_update(
                    state, query_set, key_stack[index], value_stack[index], block_start, score_scale
                )
                for state, query_set in zip(carry, query_sets)
            )
        )

    stats_done = lax.fori_loop(0, key_stack.shape[0], stats_one_block, carry)
    row_stats = tuple(((top + jnp.log(total), accum / total) for top, total, accum in stats_done))
    query_start = tuple(
        (
            jnp.zeros((query_set[2].shape[0], kv_local, group, HEAD_DIM), jnp.float32)
            for query_set in query_sets
        )
    )
    grads_start = (query_start, jnp.zeros((all_keys, 2, kv_local, HEAD_DIM), jnp.float32))
    carry = grads_start
    run_key_stack, run_value_stack, run_block_size = key_blocks(
        (
            lax.all_gather(key_heads, "ctx", axis=0, tiled=True),
            lax.all_gather(value_heads, "ctx", axis=0, tiled=True),
        )
    )

    def run_one_block(index, carry):
        query_totals, key_value_total = carry
        block_start = index * run_block_size
        slot_start = index * run_block_size
        new_totals = []
        for query_total, query_set, stats in zip(query_totals, query_sets, row_stats):
            query_total, key_value_total = grads_update(
                (query_total, key_value_total),
                query_set,
                stats,
                run_key_stack[index],
                run_value_stack[index],
                block_start,
                slot_start,
                score_scale,
            )
            new_totals.append(query_total)
        return (tuple(new_totals), key_value_total)

    query_totals, key_value_total = lax.fori_loop(0, run_key_stack.shape[0], run_one_block, carry)
    key_value_own = lax.psum_scatter(key_value_total, "ctx", scatter_dimension=0, tiled=True)
    key_grad = (key_value_own[:, 0] * score_scale).astype(jnp.bfloat16).reshape(1, rows_dev, -1)
    value_grad = key_value_own[:, 1].astype(jnp.bfloat16).reshape(1, rows_dev, -1)
    query_parts = [
        (total * score_scale).astype(jnp.bfloat16).reshape(total.shape[0], -1)
        for total in query_totals
    ]
    query_grad = query_parts[0].reshape(1, rows_dev, -1)
    local_experts = w_down.shape[0]
    experts_all = lax.axis_size(("dp", "ctx")) * local_experts
    token_rows = expert_ids.shape[0]
    capacity = min(
        token_rows,
        max(
            2,
            token_rows * TOPK * 5 // (4 * experts_all),
            (token_rows * TOPK + experts_all - 1) // experts_all,
        ),
    )
    flat_ids = expert_ids.reshape(-1)
    hits = (flat_ids[:, None] == jnp.arange(experts_all, dtype=jnp.int32)[None, :]).astype(
        jnp.int32
    )
    ranks = jnp.cumsum(hits, axis=0)
    slot_of = jnp.sum(hits * ranks, axis=1) - 1
    target = flat_ids * capacity + slot_of
    chosen = jnp.arange(experts_all * capacity, dtype=jnp.int32)[:, None] == target[None, :]
    token_pick = (
        chosen.reshape(experts_all * capacity, token_rows, TOPK).sum(axis=2).astype(jnp.bfloat16)
    )
    slot_weights = (
        jnp.dot(
            chosen.astype(jnp.bfloat16), combine.reshape(-1), preferred_element_type=jnp.float32
        )
        .astype(jnp.bfloat16)
        .reshape(experts_all, capacity)
    )
    full_rows = lax.all_gather(mixed_grad, "tp", axis=1, tiled=True)
    send_rows = (
        jnp.dot(token_pick, full_rows, preferred_element_type=jnp.float32)
        .astype(jnp.bfloat16)
        .reshape(experts_all, capacity, -1)
    )
    rows = lax.all_to_all(send_rows, ("dp", "ctx"), split_axis=0, concat_axis=0, tiled=True)
    sources = rows.shape[0] // local_experts
    row_view = rows.reshape(sources, local_experts, rows.shape[1], rows.shape[2])
    hidden = jnp.einsum("sejf,ehf->esjh", row_view, w_down, preferred_element_type=jnp.float32)
    weight_view = (
        lax.all_to_all(slot_weights, ("dp", "ctx"), split_axis=0, concat_axis=0, tiled=True)
        .reshape(sources, local_experts, -1)
        .transpose(1, 0, 2)
        .astype(jnp.float32)
    )
    hidden_grad = (hidden * weight_view[..., None]).astype(jnp.bfloat16)
    return (query_grad, key_grad, value_grad, hidden_grad)


def solution(mesh):
    placed = (
        P("dp", "ctx", "tp"),
        P("dp", "ctx", "tp"),
        P("dp", "ctx", "tp"),
        P("dp", "ctx", "tp"),
        P(("dp", "ctx"), "tp"),
        P(("dp", "ctx"), None),
        P(("dp", "ctx"), None),
        P(("dp", "ctx"), "tp", None),
    )
    return jax.shard_map(
        per_device,
        mesh=mesh,
        in_specs=placed,
        out_specs=(
            P("dp", "ctx", "tp"),
            P("dp", "ctx", "tp"),
            P("dp", "ctx", "tp"),
            P(("dp", "ctx"), None, None, "tp"),
        ),
        check_vma=False,
    )
```

profile of v0, /device:TPU:8, one launch (start us, length us, event | category | flops | bytes accessed | tf_op | source)
XLA Modules:
  0.0 960.0 jit_solution(1083310492327164624)
XLA Ops:
  11.2 19.5 %all-to-all-start.1 = ((bf16[128,1,10]{2,1,0:T(2,128)(2,1)}), bf16[128,1,10]{2,1,0:T(2,128)(2,1)S(1)}, u32[]{:S(2)}, u32[]{:S(2)}) async-start(bf16[128,1,10]{2,1,0:T(2,128)(2,1)} %all_to_all.12), calls=%async_computation.2 | async-start | bytes 131072 | tf_op jit(solution)/shard_map/all_to_all | solution.py:227
  30.9 6.7 convert_reduce_fusion
  37.6 15.4 %all_gather.13 = bf16[128,2048]{1,0:T(8,128)(2,1)S(1)} all-gather(bf16[128,512]{1,0:T(8,128)(2,1)S(1)} %copy-done.3), channel_id=1, replica_groups=mesh['dp'=4,'ctx'=32,'tp'=4] {'tp'}, dimensions={1}, use_global_device_ids=true | all-gather | bytes 655360 | tf_op jit(solution)/shard_map/all_gather | solution.py:216
  53.0 3.9 convolution_convert_fusion
  56.9 9.6 reshape.291
  66.5 24.1 %all-to-all-start = ((bf16[128,10,2048]{2,1,0:T(8,128)(2,1)}), bf16[128,10,2048]{2,1,0:T(8,128)(2,1)}, u32[]{:S(2)}, u32[]{:S(2)}) async-start(bf16[128,10,2048]{2,1,0:T(8,128)(2,1)} %reshape.291), calls=%async_computation.1 | async-start | bytes 16777216 | tf_op jit(solution)/shard_map/all_to_all | solution.py:222
  93.1 231.1 %all-gather.5.cloned.1.call-done = bf16[1,4096,128]{2,1,0:T(8,128)(2,1)} async-done(((bf16[1,128,128]{2,1,0:T(8,128)(2,1)}), bf16[1,4096,128]{2,1,0:T(8,128)(2,1)}) %all-gather.5.cloned.1.call-update) | async-done | bytes 1048592 | tf_op jit(solution)/shard_map/all_gather | solution.py:154
  324.2 237.7 %all-gather.7.cloned.1.call-done = bf16[1,4096,128]{2,1,0:T(8,128)(2,1)} async-done(((bf16[1,128,128]{2,1,0:T(8,128)(2,1)}), bf16[1,4096,128]{2,1,0:T(8,128)(2,1)}) %all-gather.7.cloned.1.call-update) | async-done | bytes 1048592 | tf_op jit(solution)/shard_map/all_gather | solution.py:155
  561.9 13.9 %while.32 = (s32[]{:T(128)}, f32[1,8,128]{2,1,0:T(8,128)S(1)}, f32[1,8,128]{2,1,0:T(8,128)S(1)}, f32[1,8,128]{2,1,0:T(8,128)S(1)}, s32[128]{0:T(128)S(1)}, /*ind...) while((s32[]{:T(128)}, f32[1,8,128]{2,1,0:T(8,128)S(1)}, ...), condition=%wide.region_6.7_spmd, body=%wide.region_0.6_spmd.sunk | while | flops 275844608 | bytes 7419675 | solution.py:142
  563.1 3.7 conditional.4
  563.3 1.4 fusion.1
  564.7 1.6 fusion
  575.8 2.2 broadcast_in_dim.67
  578.8 19.1 %while.33 = (s32[]{:T(128)}, f32[128,1,8,128]{0,3,2,1:T(8,128)}, f32[4096,2,1,128]{3,0,2,1:T(8,128)}, s32[128]{0:T(128)S(1)}, bf16[8,512,1,128]{3,1,2,0:T(8,128)...) while((s32[]{:T(128)}, f32[128,1,8,128]{0,3,2,1:T(8,128)}, ...), condition=%wide.region_10.11_spmd, body=%wide.region_7.10_spmd.sunk | while | flops 675742208 | bytes 14170433 | solution.py:178
  580.1 8.9 conditional.5
  580.2 1.6 fusion.16
  581.8 1.3 fusion.17
  583.2 1.1 convolution_bitcast_fusion.2
  584.8 2.0 fusion.21
  586.7 2.2 fusion.18
  600.1 339.9 %reduce-scatter.2.cloned.1.call-done = f32[128,2,1,128]{3,0,2,1:T(8,128)} async-done(((f32[4096,2,1,128]{3,0,2,1:T(8,128)}), f32[128,2,1,128]{3,0,2,1:T(8,128)}) %reduce-scatter.2.cloned.1.call-update) | async-done | bytes 131088 | tf_op jit(solution)/shard_map/reduce_scatter | solution.py:179
  940.0 1.5 fusion.54
  941.4 1.5 fusion.55
  942.9 10.6 %fusion.42 = bf16[1,128,10,384]{3,1,2,0:T(8,128)(2,1)} fusion(bf16[1,384,2048]{2,1,0:T(8,128)(2,1)S(1)} %copy-done, bf16[128,10,2048]{2,1,0:T(8,128)(2,1)} %all-to-all-done, f32[128,10]{0,1:T(8,128)S(1)} %copy.91), kind=kOutput, calls=%fused_computation.62 | convolution fusion | flops 2014248960 | bytes 7803904 | tf_op jit(solution)/shard_map/sejf,ehf->esjh/dot_general | solution.py:225
  (92 shorter events, 20.2 us)
Async XLA Ops:
  7.2 935.7 %copy-start = (bf16[1,384,2048]{2,1,0:T(8,128)(2,1)S(1)}, bf16[1,384,2048]{2,1,0:T(8,128)(2,1)}, u32[]{:S(2)}) copy-start(bf16[1,384,2048]{2,1,0:T(8,128)(2,1)} %param.23) | copy-start | bytes 4718596
  7.2 2.0 copy-start.5
  8.6 22.2 %copy-start.4 = (s32[128,8]{0,1:T(8,128)S(1)}, s32[128,8]{0,1:T(8,128)}, u32[]{:S(2)}) copy-start(s32[128,8]{0,1:T(8,128)} %param.21) | copy-start | bytes 12292
  8.7 28.9 %copy-start.3 = (bf16[128,512]{1,0:T(8,128)(2,1)S(1)}, bf16[128,512]{1,0:T(8,128)(2,1)}, u32[]{:S(2)}) copy-start(bf16[128,512]{1,0:T(8,128)(2,1)} %param.20) | copy-start | bytes 393220
  11.2 55.2 %all-to-all-start.1 = ((bf16[128,1,10]{2,1,0:T(2,128)(2,1)}), bf16[128,1,10]{2,1,0:T(2,128)(2,1)S(1)}, u32[]{:S(2)}, u32[]{:S(2)}) async-start(bf16[128,1,10]{2,1,0:T(2,128)(2,1)} %all_to_all.12), calls=%async_computation.2 | async-start | bytes 131072 | tf_op jit(solution)/shard_map/all_to_all | solution.py:227
  66.4 25.9 %copy-start.1 = (bf16[1,128,1024]{2,1,0:T(8,128)(2,1)S(1)}, bf16[1,128,1024]{2,1,0:T(8,128)(2,1)}, u32[]{:S(2)}) copy-start(bf16[1,128,1024]{2,1,0:T(8,128)(2,1)} %param.19) | copy-start | bytes 786436
  66.4 26.2 %copy-start.2 = (bf16[1,128,1024]{2,1,0:T(8,128)(2,1)S(1)}, bf16[1,128,1024]{2,1,0:T(8,128)(2,1)}, u32[]{:S(2)}) copy-start(bf16[1,128,1024]{2,1,0:T(8,128)(2,1)} %param.16) | copy-start | bytes 786436
  66.5 876.4 %all-to-all-start = ((bf16[128,10,2048]{2,1,0:T(8,128)(2,1)}), bf16[128,10,2048]{2,1,0:T(8,128)(2,1)}, u32[]{:S(2)}, u32[]{:S(2)}) async-start(bf16[128,10,2048]{2,1,0:T(8,128)(2,1)} %reshape.291), calls=%async_computation.1 | async-start | bytes 16777216 | tf_op jit(solution)/shard_map/all_to_all | solution.py:222
  90.6 233.6 %all-gather.5.cloned.1.call-start = ((), (), s32[]{:S(2)}) async-start(), calls=%async_computation.4 | async-start | bytes 1081344 | tf_op jit(solution)/shard_map/all_gather | solution.py:154
  91.3 470.6 %all-gather.7.cloned.1.call-start = ((), (), s32[]{:S(2)}) async-start(), calls=%async_computation.5 | async-start | bytes 1081344 | tf_op jit(solution)/shard_map/all_gather | solution.py:155
  92.1 847.9 %reduce-scatter.2.cloned.1.call-start = ((), (), s32[]{:S(2)}) async-start(), calls=%async_computation.3 | async-start | bytes 4325376 | tf_op jit(solution)/shard_map/reduce_scatter | solution.py:179
Sparse Core Ops, SparseCore 0:
  93.5 230.6 all-gather.4
  326.2 235.5 all-gather.6
  598.1 341.8 reduce-scatter.1
where the time goes:
time: 962 us; the launch traced here: 960 us
  waiting for transfers between devices  810 us (84%)
  starting transfers between devices  43.9 us (5%)
  local copies, waits for them, and re-layouts  27.5 us (3%)
  matrix products  25.2 us (3%)
  blocking collectives  15.4 us (2%)
  between operations  14 us (1%)
  other arithmetic  12.8 us (1%)
  loops' own time  11.1 us (1%)
    reduce_scatter x1, waiting for transfers between devices, per_device(): lax.psum_scatter(key_value_total, 'ctx', scatter_dimension=0, tiled=True)  340 us
    all_gather x1, waiting for transfers between devices, per_device(): lax.all_gather(value_heads, 'ctx', axis=0, tiled=True)  238 us
    all_gather x1, waiting for transfers between devices, per_device(): lax.all_gather(key_heads, 'ctx', axis=0, tiled=True)  231 us
    all_to_all x1, starting transfers between devices, per_device(): lax.all_to_all(send_rows, ('dp', 'ctx'), split_axis=0, concat_axis=0, til...  24.1 us
    all_to_all x1, starting transfers between devices, per_device(): lax.all_to_all(slot_weights, ('dp', 'ctx'), split_axis=0, concat_axis=0,...  19.5 us
  transfers between devices with their start and end apart: 5, of which 3 were waited for; matrix products, arithmetic and copies ran while one was open for 5% of the time, Pallas kernels for 0%

commit v1 on v0

v1 whole, which is shorter than its diff:
```python
import functools
import math

import jax
import jax.numpy as jnp
from jax import lax
from jax.experimental import pallas as pl
from jax.experimental.pallas import tpu as pltpu
from jax.sharding import PartitionSpec as P

MESH = pl.DeviceIdType.MESH
HEAD_DIM = 128
GROUP = 8
TOK = 128
SLOTS = 10
EXPERTS = 128
NX, NY, NL, NZ = 4, 4, 8, 16
RUN = NL * TOK
WIDE = 2 * HEAD_DIM
CHUNK = 256
ROWS = GROUP * TOK
PACK = NL * SLOTS
SCALE = HEAD_DIM**-0.5
SCALE2 = SCALE / math.log(2.0)
MASKED = -1e30
F32, BF16 = jnp.float32, jnp.bfloat16


def dot_nt(a, b):
    return lax.dot_general(a, b, (((1,), (1,)), ((), ())), preferred_element_type=F32)


def dot_nn(a, b):
    return lax.dot_general(a, b, (((1,), (0,)), ((), ())), preferred_element_type=F32)


def dot_tn(a, b):
    return lax.dot_general(a, b, (((0,), (0,)), ((), ())), preferred_element_type=F32)


def remote(src, dst, sems, where):
    return pltpu.make_async_remote_copy(
        src_ref=src,
        dst_ref=dst,
        send_sem=sems[0],
        recv_sem=sems[1],
        device_id=where,
        device_id_type=MESH,
    )


def token_targets(ids_ref, comb_ref):
    expert = lax.broadcasted_iota(jnp.int32, (EXPERTS, TOK), 0)
    hits = jnp.zeros((EXPERTS, TOK), F32)
    for k in range(8):
        hits += jnp.where(ids_ref[k : k + 1, :] == expert, 1.0, 0.0)
    rows = lax.broadcasted_iota(jnp.int32, (TOK, TOK), 0)
    cols = lax.broadcasted_iota(jnp.int32, (TOK, TOK), 1)
    before = jnp.where(rows < cols, 1.0, 0.0).astype(BF16)
    ranks = dot_nn(hits.astype(BF16), before)
    out = []
    for k in range(8):
        ids = ids_ref[k : k + 1, :]
        slot = jnp.sum(jnp.where(ids == expert, ranks, 0.0), axis=0, keepdims=True)
        out.append(ids.astype(F32) * float(SLOTS) + slot)
    return jnp.concatenate(out + [comb_ref[...]], axis=0)


def kernel(
    q_ref, do_ref, k_ref, v_ref, mg_ref, ids_ref, comb_ref, w_ref,
    dq_ref, dk_ref, dv_ref, hid_ref,
    kv, tg, rows, snd, rcv, qs, dos, stat, dqt, dkv, xs1, xr1, xs2, xr2, zs, zr,
    ring_s, ring_r, kz_s, kz_r, tz_s, tz_r, xf_s, xf_r, xh_s, xh_r, xb_s, xb_r, xt_s, xt_r,
    a2a_s, a2a_r, core_s, core_r, r1_s, r1_r, r2_s, r2_r, rz_s, rz_r,
):
    y = lax.axis_index("dp")
    c = lax.axis_index("ctx")
    tp = lax.axis_index("tp")
    x, zl = c // NL, c % NL
    zh, core = tp // 2, tp % 2
    z = zh * NL + zl
    plane = y * NX + x

    def at(ax, ay, az, acore):
        return (ay, ax * NL + az % NL, (az // NL) * 2 + acore)

    z_up = at(x, y, (z + 1) % NZ, core)
    z_down = at(x, y, (z + NZ - 1) % NZ, core)
    x_up = at((x + 1) % NX, y, z, core)
    x_down = at((x + NX - 1) % NX, y, z, core)
    twin = at(x, y, z, 1 - core)

    def plane_dev(d):
        return at(d % NX, d // NX, z, core)

    def line_dev(j):
        return at(x, y, zh * NL + j, core)

    barrier = pltpu.get_barrier_semaphore()

    def greet(where):
        pl.semaphore_signal(barrier, inc=1, device_id=where, device_id_type=MESH)

    greet(z_up)
    greet(z_down)
    greet(twin)

    @pl.loop(1, 16)
    def _(i):
        greet(plane_dev((plane + i) % 16))

    @pl.loop(1, NL)
    def _(i):
        greet(line_dev((zl + i) % NL))

    kv[c, :, :HEAD_DIM] = k_ref[...]
    kv[c, :, HEAD_DIM:] = v_ref[...]
    rows[z] = mg_ref[...]
    tg[zl] = token_targets(ids_ref, comb_ref)
    for h in range(GROUP):
        qs[pl.ds(h * TOK, TOK), :] = q_ref[:, h * HEAD_DIM : (h + 1) * HEAD_DIM]
        dos[pl.ds(h * TOK, TOK), :] = do_ref[:, h * HEAD_DIM : (h + 1) * HEAD_DIM]
    pl.semaphore_wait(barrier, 3 + 15 + 7)

    half = (pl.ds(0, TOK // 2), pl.ds(TOK // 2, TOK // 2))

    def ring_copy(way, step, part, src):
        ref = rows.at[src, half[part]]
        return remote(
            ref, ref, (ring_s.at[way, part, step], ring_r.at[way, part, step]), (z_up, z_down)[way]
        )

    def kz_copy(way, step, src):
        ref = kv.at[x * NL + src]
        return remote(ref, ref, (kz_s.at[way, step], kz_r.at[way, step]), (z_up, z_down)[way])

    def tz_copy(way, step, src):
        ref = tg.at[src]
        return remote(ref, ref, (tz_s.at[way, step], tz_r.at[way, step]), (z_up, z_down)[way])

    def xf_copy(g, j):
        ref = kv.at[g * NL + j]
        return remote(ref, ref, (xf_s.at[j], xf_r.at[j]), x_up)

    def xh_copy(g, j):
        ref = kv.at[g * NL + j, half[0]]
        return remote(ref, ref, (xh_s.at[j], xh_r.at[j]), x_up)

    def xb_copy(part, g, j):
        ref = kv.at[g * NL + j, half[part]]
        return remote(ref, ref, (xb_s.at[part, j], xb_r.at[part, j]), x_down)

    def xt_copy(g, j):
        ref = kv.at[g * NL + j, half[1]]
        return remote(ref, ref, (xt_s.at[j], xt_r.at[j]), x_down)

    def x_send(j):
        @pl.when(x <= 2)
        def _():
            xf_copy(x, j).start()

        @pl.when(x == 0)
        def _():
            xb_copy(0, x, j).start()

        @pl.when(x <= 1)
        def _():
            xb_copy(1, x, j).start()

    x_send(zl)

    @pl.loop(0, NL)
    def _(s):
        up_src, down_src = zl - s, zl + s

        @pl.when((zl < NL - 1) & (up_src >= 0))
        def _():
            kz_copy(0, s, up_src).start()
            tz_copy(0, s, up_src).start()

        @pl.when((zl > 0) & (down_src < NL))
        def _():
            kz_copy(1, s, down_src).start()
            tz_copy(1, s, down_src).start()

        f_src, b_src = (z + NZ - s) % NZ, (z + s) % NZ
        ring_copy(0, s, 0, f_src).start()
        ring_copy(1, s, 1, b_src).start()

        @pl.when(s < NL - 1)
        def _():
            ring_copy(0, s, 1, f_src).start()
            ring_copy(1, s, 0, b_src).start()

        @pl.when(up_src >= 1)
        def _():
            kz_copy(0, s, up_src - 1).wait_recv()
            tz_copy(0, s, up_src - 1).wait_recv()
            x_send(up_src - 1)

        @pl.when(down_src < NL - 1)
        def _():
            kz_copy(1, s, down_src + 1).wait_recv()
            tz_copy(1, s, down_src + 1).wait_recv()
            x_send(down_src + 1)

        f_got, b_got = (z + NZ - s - 1) % NZ, (z + s + 1) % NZ
        ring_copy(0, s, 0, f_got).wait_recv()
        ring_copy(1, s, 1, b_got).wait_recv()

        @pl.when(s < NL - 1)
        def _():
            ring_copy(0, s, 1, f_got).wait_recv()
            ring_copy(1, s, 0, b_got).wait_recv()

    @pl.loop(0, NL)
    def _(j):
        @pl.when(x >= 1)
        def _():
            xf_copy(x - 1, j).wait_recv()

        @pl.when((x == 1) | (x == 2))
        def _():
            xh_copy(x - 1, j).start()

        @pl.when(x == 3)
        def _():
            xb_copy(0, 0, j).wait_recv()

        @pl.when((x == 3) | (x == 0))
        def _():
            g = (x + 1) % NX
            xb_copy(1, g, j).wait_recv()
            xt_copy(g, j).start()

    pick_row = lax.broadcasted_iota(jnp.int32, (16, TOK), 0)

    def send_copy(d):
        return remote(
            snd.at[d], rcv.at[core, plane], (a2a_s.at[d], a2a_r.at[plane]), plane_dev(d)
        )

    def got_copy(d):
        return remote(
            snd.at[d], rcv.at[core, d], (a2a_s.at[d], a2a_r.at[d]), plane_dev(d)
        )

    def twin_copy(d):
        return remote(
            rcv.at[core, d], rcv.at[core, d], (core_s.at[d], core_r.at[d]), twin
        )

    def twin_got(d):
        return remote(
            rcv.at[1 - core, d], rcv.at[1 - core, d], (core_s.at[d], core_r.at[d]), twin
        )

    @pl.loop(1, 17)
    def _(i):
        d = (plane + i) % 16
        expert = (d // NX) * (NX * NL) + (d % NX) * NL + zl
        columns = []
        for b in range(NL):
            first = (b * SLOTS) // 8 * 8
            place = pick_row + (first - b * SLOTS)
            inside = (place >= 0) & (place < SLOTS)
            key = jnp.where(inside, expert * SLOTS + place, -1).astype(F32)
            window = jnp.zeros((16, TOK), F32)
            for k in range(8):
                window += jnp.where(tg[b, k : k + 1, :] == key, tg[b, 8 + k : 9 + k, :], 0.0)
            pieces = [window]
            if first > 0:
                pieces = [jnp.zeros((first, TOK), F32)] + pieces
            if first + 16 < PACK:
                pieces = pieces + [jnp.zeros((PACK - first - 16, TOK), F32)]
            columns.append(jnp.concatenate(pieces, axis=0).astype(BF16))
        pick = jnp.concatenate(columns, axis=1)
        for part in range(2):
            source = rows[part * NL : (part + 1) * NL].reshape(RUN, 512)
            picked = dot_nn(pick, source).astype(BF16)
            snd[d, :, part * 512 : (part + 1) * 512] = picked

        @pl.when(i < 16)
        def _():
            send_copy(d).start()

    rcv[core, plane] = snd[plane]
    twin_copy(plane).start()

    @pl.when(x >= 2)
    def _():
        @pl.loop(0, NL)
        def _(j):
            xh_copy(x - 2, j).wait_recv()
            xt_copy(x - 2, j).wait_recv()

    lane = lax.broadcasted_iota(jnp.int32, (1, ROWS), 1)
    query_place = zl * TOK + lane % TOK

    def scores(g, i, masked):
        block = kv[pl.ds(g * NL + i * (CHUNK // TOK), CHUNK // TOK)].reshape(CHUNK, WIDE)
        keys, values = block[:, :HEAD_DIM], block[:, HEAD_DIM:]
        s = dot_nt(keys, qs[...]) * SCALE2
        if masked:
            place = i * CHUNK + lax.broadcasted_iota(jnp.int32, (CHUNK, ROWS), 0)
            s = jnp.where(place <= query_place, s, MASKED)
        return keys, s, dot_nt(values, dos[...])

    def stats_group(g, masked):
        @pl.loop(0, RUN // CHUNK)
        def _(i):
            _, s, dp = scores(g, i, masked)
            top = stat[0:1, :]
            new_top = jnp.maximum(top, jnp.max(s, axis=0, keepdims=True))
            e = jnp.exp2(s - new_top)
            shrink = jnp.exp2(top - new_top)
            stat[0:1, :] = new_top
            stat[1:2, :] = stat[1:2, :] * shrink + jnp.sum(e, axis=0, keepdims=True)
            stat[2:3, :] = stat[2:3, :] * shrink + jnp.sum(e * dp, axis=0, keepdims=True)

    stat[0:1, :] = jnp.full((1, ROWS), MASKED, F32)
    stat[1:3, :] = jnp.zeros((2, ROWS), F32)
    stats_group(x, True)

    @pl.loop(0, x)
    def _(g):
        stats_group(g, False)

    stat[2:3, :] = stat[2:3, :] / stat[1:2, :]
    stat[0:1, :] = stat[0:1, :] + jnp.log2(stat[1:2, :])
    dqt[...] = jnp.zeros_like(dqt)

    def grads_group(g, masked):
        @pl.loop(0, RUN // CHUNK)
        def _(i):
            keys, s, dp = scores(g, i, masked)
            p = jnp.exp2(s - stat[0:1, :])
            ds = (p * (dp - stat[2:3, :])).astype(BF16)
            here = pl.ds(pl.multiple_of(i * CHUNK, CHUNK), CHUNK)
            dkv[g, here, HEAD_DIM:] = dot_nn(p.astype(BF16), dos[...])
            dkv[g, here, :HEAD_DIM] = dot_nn(ds, qs[...])
            dqt[...] += dot_tn(keys, ds)

    def r1_copy(way):
        return remote(
            xs1.at[way], xr1.at[way], (r1_s.at[way], r1_r.at[way]), (x_up, x_down)[way]
        )

    def r2_copy(way, part, src=None):
        ref = xs2.at[way, part] if src is None else src
        return remote(
            ref, xr2.at[way, part], (r2_s.at[way, part], r2_r.at[way, part]), (x_up, x_down)[way]
        )

    first, second = pl.ds(0, RUN // 2), pl.ds(RUN // 2, RUN // 2)

    @pl.when(x >= 2)
    def _():
        grads_group(x - 2, False)
        xs1[0] = dkv[x - 2, first, :].astype(BF16)
        xs1[1] = dkv[x - 2, second, :].astype(BF16)
        r1_copy(0).start()
        r1_copy(1).start()

    @pl.when(x == 3)
    def _():
        grads_group(0, False)

    @pl.when(x >= 1)
    def _():
        grads_group(x - 1, False)
        xs2[1, 0] = dkv[x - 1, first, :].astype(BF16)
        r2_copy(1, 0).start()

    @pl.when(x == 3)
    def _():
        xs2[0, 1] = dkv[0, second, :].astype(BF16)
        r2_copy(0, 1).start()
        xs2[1, 1] = dkv[2, second, :].astype(BF16)
        r2_copy(1, 1).start()
        r1_copy(0).wait_recv()
        xs2[0, 0] = (dkv[0, first, :] + xr1[0].astype(F32)).astype(BF16)
        r2_copy(0, 0).start()

    @pl.when((x == 1) | (x == 2))
    def _():
        r1_copy(1).wait_recv()
        xs2[1, 1] = (dkv[x - 1, second, :] + xr1[1].astype(F32)).astype(BF16)
        r2_copy(1, 1).start()

    @pl.when(x == 0)
    def _():
        r1_copy(0).wait_recv()
        r2_copy(0, 0, xr1.at[0]).start()

    grads_group(x, True)
    for h in range(GROUP):
        here = slice(h * TOK, (h + 1) * TOK)
        dq_ref[:, here] = (dqt[:, here].T * SCALE).astype(BF16)

    @pl.loop(1, 16)
    def _(i):
        d = (plane + 16 - i) % 16
        got_copy(d).wait_recv()
        twin_copy(d).start()

    @pl.when(x <= 2)
    def _():
        r2_copy(1, 0).wait_recv()
        dkv[x, first, :] += xr2[1, 0].astype(F32)
        r2_copy(1, 1).wait_recv()
        dkv[x, second, :] += xr2[1, 1].astype(F32)

    @pl.when(x <= 1)
    def _():
        r2_copy(0, 0).wait_recv()
        dkv[x, first, :] += xr2[0, 0].astype(F32)

    @pl.when(x == 0)
    def _():
        r2_copy(0, 1).wait_recv()
        dkv[x, second, :] += xr2[0, 1].astype(F32)

    def rz_send(j):
        return remote(zs.at[j], zr.at[zl], (rz_s.at[j], rz_r.at[zl]), line_dev(j))

    def rz_got(j):
        return remote(zs.at[j], zr.at[j], (rz_s.at[j], rz_r.at[j]), line_dev(j))

    @pl.loop(1, NL)
    def _(i):
        j = (zl + i) % NL
        zs[j] = dkv[x, pl.ds(pl.multiple_of(j * TOK, TOK), TOK), :].astype(BF16)
        rz_send(j).start()

    twin_got(plane).wait_recv()

    @pl.loop(1, 16)
    def _(i):
        twin_got((plane + 16 - i) % 16).wait_recv()

    @pl.loop(0, 4)
    def _(i):
        total = jnp.zeros((4 * PACK, w_ref.shape[0]), F32)
        for side in range(2):
            for part in range(2):
                at_feature = (part * 2 + side) * 512
                left = rcv[side, pl.ds(i * 4, 4), :, part * 512 : (part + 1) * 512]
                total += dot_nt(
                    left.reshape(4 * PACK, 512), w_ref[:, at_feature : at_feature + 512]
                )
        for b in range(4 * NL):
            hid_ref[i * (4 * NL) + b] = total[b * SLOTS : (b + 1) * SLOTS, :].astype(BF16)

    @pl.loop(1, NL)
    def _(i):
        j = (zl + i) % NL
        rz_got(j).wait_recv()
        dkv[x, pl.ds(pl.multiple_of(zl * TOK, TOK), TOK), :] += zr[j].astype(F32)

    own = dkv[x, pl.ds(pl.multiple_of(zl * TOK, TOK), TOK), :]
    dk_ref[...] = (own[:, :HEAD_DIM] * SCALE).astype(BF16)
    dv_ref[...] = own[:, HEAD_DIM:].astype(BF16)

    @pl.loop(0, NL)
    def _(s):
        @pl.when((zl < NL - 1) & (zl - s >= 0))
        def _():
            kz_copy(0, s, zl - s).wait_send()
            tz_copy(0, s, zl - s).wait_send()

        @pl.when((zl > 0) & (zl + s < NL))
        def _():
            kz_copy(1, s, zl + s).wait_send()
            tz_copy(1, s, zl + s).wait_send()

        ring_copy(0, s, 0, (z + NZ - s) % NZ).wait_send()
        ring_copy(1, s, 1, (z + s) % NZ).wait_send()

        @pl.when(s < NL - 1)
        def _():
            ring_copy(0, s, 1, (z + NZ - s) % NZ).wait_send()
            ring_copy(1, s, 0, (z + s) % NZ).wait_send()

        @pl.when(x <= 2)
        def _():
            xf_copy(x, s).wait_send()

        @pl.when(x == 0)
        def _():
            xb_copy(0, x, s).wait_send()

        @pl.when(x <= 1)
        def _():
            xb_copy(1, x, s).wait_send()

        @pl.when((x == 1) | (x == 2))
        def _():
            xh_copy(x - 1, s).wait_send()

        @pl.when((x == 3) | (x == 0))
        def _():
            xt_copy((x + 1) % NX, s).wait_send()

    twin_copy(plane).wait_send()

    @pl.loop(1, 16)
    def _(i):
        d = (plane + i) % 16
        send_copy(d).wait_send()
        twin_copy(d).wait_send()

    @pl.when(x >= 2)
    def _():
        r1_copy(0).wait_send()
        r1_copy(1).wait_send()

    @pl.when(x >= 1)
    def _():
        r2_copy(1, 0).wait_send()
        r2_copy(1, 1).wait_send()

    @pl.when((x == 3) | (x == 0))
    def _():
        r2_copy(0, 0).wait_send()

    @pl.when(x == 3)
    def _():
        r2_copy(0, 1).wait_send()

    @pl.loop(1, NL)
    def _(i):
        rz_send((zl + i) % NL).wait_send()


def per_device(queries, keys, values, out_grad, mixed_grad, expert_ids, combine, w_down):
    ids = expert_ids.T
    weights = combine.T.astype(F32)
    vmem = pl.BlockSpec(memory_space=pltpu.VMEM)
    dma = pltpu.SemaphoreType.DMA
    hid = w_down.shape[1]
    shapes = (
        jax.ShapeDtypeStruct((TOK, ROWS), BF16),
        jax.ShapeDtypeStruct((TOK, HEAD_DIM), BF16),
        jax.ShapeDtypeStruct((TOK, HEAD_DIM), BF16),
        jax.ShapeDtypeStruct((EXPERTS, SLOTS, hid), BF16),
    )
    scratch = [
        pltpu.VMEM((NX * NL, TOK, WIDE), BF16),
        pltpu.VMEM((NL, 16, TOK), F32),
        pltpu.VMEM((NZ, TOK, 512), BF16),
        pltpu.VMEM((16, PACK, 1024), BF16),
        pltpu.VMEM((2, 16, PACK, 1024), BF16),
        pltpu.VMEM((ROWS, HEAD_DIM), BF16),
        pltpu.VMEM((ROWS, HEAD_DIM), BF16),
        pltpu.VMEM((8, ROWS), F32),
        pltpu.VMEM((HEAD_DIM, ROWS), F32),
        pltpu.VMEM((NX, RUN, WIDE), F32),
        pltpu.VMEM((2, RUN // 2, WIDE), BF16),
        pltpu.VMEM((2, RUN // 2, WIDE), BF16),
        pltpu.VMEM((2, 2, RUN // 2, WIDE), BF16),
        pltpu.VMEM((2, 2, RUN // 2, WIDE), BF16),
        pltpu.VMEM((NL, TOK, WIDE), BF16),
        pltpu.VMEM((NL, TOK, WIDE), BF16),
    ]
    for shape in (
        (2, 2, NL), (2, NL), (2, NL), (NL,), (NL,), (2, NL), (NL,),
        (16,), (16,), (2,), (2, 2), (NL,),
    ):
        scratch += [dma(shape), dma(shape)]
    dq, dk, dv, hidden = pl.pallas_call(
        kernel,
        out_shape=shapes,
        in_specs=[vmem] * 8,
        out_specs=(vmem,) * 4,
        scratch_shapes=scratch,
        compiler_params=pltpu.CompilerParams(
            collective_id=0, has_side_effects=True, vmem_limit_bytes=56 * 1024 * 1024
        ),
        name="layer_backward",
    )(queries[0], out_grad[0], keys[0], values[0], mixed_grad, ids, weights, w_down[0])
    return dq[None], dk[None], dv[None], hidden[None]


def solution(mesh):
    placed = (
        P("dp", "ctx", "tp"),
        P("dp", "ctx", "tp"),
        P("dp", "ctx", "tp"),
        P("dp", "ctx", "tp"),
        P(("dp", "ctx"), "tp"),
        P(("dp", "ctx"), None),
        P(("dp", "ctx"), None),
        P(("dp", "ctx"), "tp", None),
    )
    return jax.shard_map(
        per_device,
        mesh=mesh,
        in_specs=placed,
        out_specs=(
            P("dp", "ctx", "tp"),
            P("dp", "ctx", "tp"),
            P("dp", "ctx", "tp"),
            P(("dp", "ctx"), None, None, "tp"),
        ),
        check_vma=False,
    )
```

time: 962 us -> 130 us (0.14)
  the two profiles are of different devices: /device:TPU:8 before, /device:TPU:60 now
where the time goes in v1:
time: 130 us
  Pallas kernels  124 us (95%)
  local copies, waits for them, and re-layouts  4.55 us (4%)
    pallas_call x1, Pallas kernels, per_device(): pl.pallas_call(kernel, out_shape=shapes, in_specs=[vmem] * 8, out_specs=(...  124 us
    unnamed x10, local copies, waits for them, and re-layouts  4.55 us

profile of v1, /device:TPU:60, one launch (start us, length us, event | category | flops | bytes accessed | tf_op | source)
XLA Modules:
  0.0 130.1 jit_solution(19127696801506595)
XLA Ops:
  0.6 1.3 convert_bitcast_fusion.comb_ref
  1.9 123.6 %layer_backward.1 = (bf16[128,1024]{1,0:T(8,128)(2,1)}, bf16[128,128]{1,0:T(8,128)(2,1)}, bf16[128,128]{1,0:T(8,128)(2,1)}, bf16[128,10,384]{2,1,0:T(8,128)(2,1)}) custom-call(bf16[128,1024]{1,0:T(8,128)(2,1)} %bitcast.14, bf16[128,1024]{1,0:T(8,128)(2,1)} %bitcast.15, bf16[128,128]{1,0:T(8,128)(2,1)} %bitcast.17, bf16[128,128]{1,0:T(8,128)(2,1)} %bitcast.18, ...), custom_call_target="tpu_custom_call" | custom-call | tf_op jit(solution)/shard_map/layer_backward/pallas_call | solution.py:571
  125.5 0.0 copy-start
  125.5 0.0 copy-start.2
  125.5 0.0 copy-start.1
  125.5 2.6 %copy.12 = bf16[1,128,10,384]{3,1,2,0:T(8,128)(2,1)} copy(bf16[1,128,10,384]{3,2,1,0:T(8,128)(2,1)} %bitcast.13) | data formatting | bytes 1966080
  128.1 0.0 copy-done
  128.1 0.7 copy.16
  128.8 0.0 copy-done.2
  128.9 0.6 copy.17
  129.5 0.0 copy-done.1
  129.5 0.6 copy.18
Async XLA Ops:
  125.5 2.6 %copy-start = (bf16[128,1024]{1,0:T(8,128)(2,1)S(1)}, bf16[128,1024]{1,0:T(8,128)(2,1)}, u32[]{:S(2)}) copy-start(bf16[128,1024]{1,0:T(8,128)(2,1)} %get-tuple-element.8) | copy-start | bytes 786436
  125.5 3.3 %copy-start.2 = (bf16[128,128]{1,0:T(8,128)(2,1)S(1)}, bf16[128,128]{1,0:T(8,128)(2,1)}, u32[]{:S(2)}) copy-start(bf16[128,128]{1,0:T(8,128)(2,1)} %get-tuple-element.9) | copy-start | bytes 98308
  125.5 3.9 %copy-start.1 = (bf16[128,128]{1,0:T(8,128)(2,1)S(1)}, bf16[128,128]{1,0:T(8,128)(2,1)}, u32[]{:S(2)}) copy-start(bf16[128,128]{1,0:T(8,128)(2,1)} %get-tuple-element.10) | copy-start | bytes 98308

commit v2 on v1

v2 whole, which is shorter than its diff:
```python
import functools
import math

import jax
import jax.numpy as jnp
from jax import lax
from jax.experimental import pallas as pl
from jax.experimental.pallas import tpu as pltpu
from jax.sharding import PartitionSpec as P

MESH = pl.DeviceIdType.MESH
HEAD_DIM = 128
GROUP = 8
TOK = 128
SLOTS = 10
EXPERTS = 128
NX, NY, NL, NZ = 4, 4, 8, 16
RUN = NL * TOK
WIDE = 2 * HEAD_DIM
CHUNK = 256
ROWS = GROUP * TOK
PACK = NL * SLOTS
SIDE = 16
PART = 512
SCALE = HEAD_DIM**-0.5
SCALE2 = SCALE / math.log(2.0)
MASKED = -1e30
F32, BF16 = jnp.float32, jnp.bfloat16


def dot_nt(a, b):
    return lax.dot_general(a, b, (((1,), (1,)), ((), ())), preferred_element_type=F32)


def dot_nn(a, b):
    return lax.dot_general(a, b, (((1,), (0,)), ((), ())), preferred_element_type=F32)


def dot_tn(a, b):
    return lax.dot_general(a, b, (((0,), (0,)), ((), ())), preferred_element_type=F32)


def remote(src, dst, sems, where):
    return pltpu.make_async_remote_copy(
        src_ref=src,
        dst_ref=dst,
        send_sem=sems[0],
        recv_sem=sems[1],
        device_id=where,
        device_id_type=MESH,
    )


def token_targets(ids, weights):
    expert = lax.broadcasted_iota(jnp.int32, (EXPERTS, TOK), 0).astype(F32)
    hits = jnp.zeros((EXPERTS, TOK), F32)
    for k in range(8):
        hits += jnp.where(ids[k : k + 1, :] == expert, 1.0, 0.0)
    rows = lax.broadcasted_iota(jnp.int32, (TOK, TOK), 0)
    cols = lax.broadcasted_iota(jnp.int32, (TOK, TOK), 1)
    before = jnp.where(rows < cols, 1.0, 0.0).astype(BF16)
    ranks = dot_nn(hits.astype(BF16), before)
    slots = [
        jnp.sum(jnp.where(ids[k : k + 1, :] == expert, ranks, 0.0), axis=0, keepdims=True)
        for k in range(8)
    ]
    slots = jnp.concatenate(slots, axis=0)
    top = jnp.concatenate([ids, slots, weights, jnp.zeros_like(ids)], axis=1)
    return jnp.concatenate([top, jnp.zeros_like(top)], axis=0).astype(BF16)


def kernel(
    q_ref, do_ref, k_ref, v_ref, mg_ref, ids_ref, comb_ref, w_ref,
    dq_ref, dk_ref, dv_ref, hid_ref,
    kv, rows, picks, snd, rcv, qs, dos, stat, dqt, dkv, xs1, xr1, xs2, xr2, zs, zr,
    ring_s, ring_r, kz_s, kz_r, xf_s, xf_r, xh_s, xh_r, xb_s, xb_r, xt_s, xt_r,
    a2a_s, a2a_r, all_s, all_r, core_s, core_r, r1_s, r1_r, r2_s, r2_r, rz_s, rz_r,
):
    y = lax.axis_index("dp")
    c = lax.axis_index("ctx")
    tp = lax.axis_index("tp")
    x, zl = c // NL, c % NL
    zh, core = tp // 2, tp % 2
    z = zh * NL + zl
    plane = y * NX + x

    def at(ax, ay, az, acore):
        return (ay, ax * NL + az % NL, (az // NL) * 2 + acore)

    z_up = at(x, y, (z + 1) % NZ, core)
    z_down = at(x, y, (z + NZ - 1) % NZ, core)
    x_up = at((x + 1) % NX, y, z, core)
    x_down = at((x + NX - 1) % NX, y, z, core)
    twin = at(x, y, z, 1 - core)

    def plane_dev(d):
        return at(d % NX, d // NX, z, core)

    def line_dev(j):
        return at(x, y, zh * NL + j, core)

    barrier = pltpu.get_barrier_semaphore()

    def greet(where):
        pl.semaphore_signal(barrier, inc=1, device_id=where, device_id_type=MESH)

    greet(z_up)
    greet(z_down)
    greet(twin)

    @pl.loop(1, 16)
    def _(i):
        greet(plane_dev((plane + i) % 16))

    @pl.loop(1, NL)
    def _(i):
        greet(line_dev((zl + i) % NL))

    kv[c, :, :HEAD_DIM] = k_ref[...]
    kv[c, :, HEAD_DIM:] = v_ref[...]
    rows[8, pl.ds(SIDE, TOK), :] = mg_ref[...]
    rows[8, pl.ds(0, SIDE), :] = token_targets(
        ids_ref[...].astype(F32), comb_ref[...].astype(F32)
    )
    for h in range(GROUP):
        qs[pl.ds(h * TOK, TOK), :] = q_ref[:, h * HEAD_DIM : (h + 1) * HEAD_DIM]
        dos[pl.ds(h * TOK, TOK), :] = do_ref[:, h * HEAD_DIM : (h + 1) * HEAD_DIM]
    stat[0:1, :] = jnp.full((1, ROWS), MASKED, F32)
    stat[1:3, :] = jnp.zeros((2, ROWS), F32)
    pl.semaphore_wait(barrier, 3 + 15 + 7)

    half = (pl.ds(0, TOK // 2), pl.ds(TOK // 2, TOK // 2))
    whole = pl.ds(0, SIDE + TOK // 2)
    piece = (pl.ds(SIDE, TOK // 2), pl.ds(SIDE + TOK // 2, TOK // 2))

    def ring(way, part, s, op):
        near = (8 - s, 8 + s)[way]
        far = (7 - s, (9 + s) % NZ)[way]
        last = (3, 2)[way]

        def copy(span):
            if op != "wait_recv":
                source, target = rows.at[near, span], rows.at[far, span]
            else:
                source, target = rows.at[far, span], rows.at[far, span]
            sems = (ring_s.at[way, part, s], ring_r.at[way, part, s])
            getattr(remote(source, target, sems, (z_up, z_down)[way]), op)()

        if part == 1:
            copy(piece[1])
        else:
            pl.when(s <= last)(lambda: copy(whole))
            pl.when(s > last)(lambda: copy(piece[0]))

    def kz_copy(way, step, src):
        ref = kv.at[x * NL + src]
        return remote(ref, ref, (kz_s.at[way, step], kz_r.at[way, step]), (z_up, z_down)[way])

    def xf_copy(g, j):
        ref = kv.at[g * NL + j]
        return remote(ref, ref, (xf_s.at[j], xf_r.at[j]), x_up)

    def xh_copy(g, j):
        ref = kv.at[g * NL + j, half[0]]
        return remote(ref, ref, (xh_s.at[j], xh_r.at[j]), x_up)

    def xb_copy(part, g, j):
        ref = kv.at[g * NL + j, half[part]]
        return remote(ref, ref, (xb_s.at[part, j], xb_r.at[part, j]), x_down)

    def xt_copy(g, j):
        ref = kv.at[g * NL + j, half[1]]
        return remote(ref, ref, (xt_s.at[j], xt_r.at[j]), x_down)

    def x_send(j):
        @pl.when(x <= 2)
        def _():
            xf_copy(x, j).start()

        @pl.when(x == 0)
        def _():
            xb_copy(0, x, j).start()

        @pl.when(x <= 1)
        def _():
            xb_copy(1, x, j).start()

    lane = lax.broadcasted_iota(jnp.int32, (1, ROWS), 1) % TOK

    def scores(slot, count, first):
        size = count * TOK
        block = kv[pl.ds(slot, count)].reshape(size, WIDE)
        keys, values = block[:, :HEAD_DIM], block[:, HEAD_DIM:]
        s = dot_nt(keys, qs[...]) * SCALE2
        if first is not None:
            place = lax.broadcasted_iota(jnp.int32, (size, ROWS), 0)
            s = jnp.where(place <= lane + first, s, MASKED)
        return keys, s, dot_nt(values, dos[...])

    def stats(slot, count, first=None):
        _, s, dp = scores(slot, count, first)
        top = stat[0:1, :]
        new_top = jnp.maximum(top, jnp.max(s, axis=0, keepdims=True))
        e = jnp.exp2(s - new_top)
        shrink = jnp.exp2(top - new_top)
        stat[0:1, :] = new_top
        stat[1:2, :] = stat[1:2, :] * shrink + jnp.sum(e, axis=0, keepdims=True)
        stat[2:3, :] = stat[2:3, :] * shrink + jnp.sum(e * dp, axis=0, keepdims=True)

    def x_pass(j):
        @pl.when((j >= 0) & (j < NL))
        def _():
            @pl.when(x >= 1)
            def _():
                xf_copy(x - 1, j).wait_recv()

            @pl.when((x == 1) | (x == 2))
            def _():
                xh_copy(x - 1, j).start()

            @pl.when(x == 3)
            def _():
                xb_copy(0, 0, j).wait_recv()

            @pl.when((x == 3) | (x == 0))
            def _():
                xb_copy(1, (x + 1) % NX, j).wait_recv()
                xt_copy((x + 1) % NX, j).start()

            @pl.when(x >= 1)
            def _():
                stats((x - 1) * NL + j, 1)

            @pl.when(x == 3)
            def _():
                stats(j, 1)

    pick_row = lax.broadcasted_iota(jnp.int32, (16, TOK), 0)
    pick_block = lax.broadcasted_iota(jnp.int32, (NL, TOK), 0)

    def make_pick(r):
        d = (plane + r + 1) % 16
        expert = (d // NX) * (NX * NL) + (d % NX) * NL + zl
        key = jnp.where(pick_row < SLOTS, expert * SLOTS + pick_row, -1).astype(F32)
        columns = []
        for n in range(NL):
            named = rows[4 + n, pl.ds(0, SIDE), :].astype(F32)
            target = named[:8, :TOK] * float(SLOTS) + named[:8, TOK : 2 * TOK]
            weight = named[:8, 2 * TOK : 3 * TOK]
            window = jnp.zeros((16, TOK), F32)
            for k in range(8):
                window += jnp.where(target[k : k + 1, :] == key, weight[k : k + 1, :], 0.0)
            mine = pick_block == (zl + 4 + n) % NL
            column = [jnp.where(mine, window[i : i + 1, :], 0.0) for i in range(SLOTS)]
            columns.append(jnp.concatenate(column, axis=0).astype(BF16))
        picks[r] = jnp.concatenate(columns, axis=1)

    def a2a_out(w, r):
        return remote(
            snd.at[w, r], rcv.at[core, w, plane], (a2a_s.at[w, r], a2a_r.at[w, plane]),
            plane_dev((plane + r + 1) % 16),
        )

    def a2a_in(w, d):
        return remote(
            snd.at[w, 0], rcv.at[core, w, d], (a2a_s.at[w, 0], a2a_r.at[w, d]), plane_dev(d)
        )

    def pack_rows(w, n):
        if w == 0:
            @pl.loop(0, 4)
            def _(i):
                make_pick(n * 4 + i)

        total = jnp.zeros((4 * PACK, PART), F32)
        for m, start in enumerate(((4, 8), (12, 0))[w]):
            source = rows[start : start + 4, SIDE:, :].reshape(4 * TOK, PART)
            chosen = picks[pl.ds(n * 4, 4), :, m * 4 * TOK : (m + 1) * 4 * TOK]
            total += dot_nn(chosen.reshape(4 * PACK, 4 * TOK), source)
        snd[w, pl.ds(n * 4, 4)] = total.astype(BF16).reshape(4, PACK, PART)

        @pl.when(n == 3)
        def _():
            rcv[core, w, plane] = snd[w, 15]

    def launch_rows(w, n):
        @pl.loop(0, 4)
        def _(i):
            r = n * 4 + i

            @pl.when(r < 15)
            def _():
                a2a_out(w, r).start()

    @pl.when(zl < NL - 1)
    def _():
        kz_copy(0, 0, zl).start()

    @pl.when(zl > 0)
    def _():
        kz_copy(1, 0, zl).start()

    x_send(zl)
    ring(0, 0, 0, "start")
    ring(1, 1, 0, "start")
    ring(0, 1, 0, "start")
    ring(1, 0, 0, "start")
    stats(c, 1, 0)

    @pl.loop(0, NL + 1)
    def _(s):
        below, above = zl - 1 - s, zl + 1 + s

        @pl.when(below >= 0)
        def _():
            kz_copy(0, s, below).wait_recv()

            @pl.when(zl < NL - 1)
            def _():
                kz_copy(0, s + 1, below).start()

        @pl.when(above < NL)
        def _():
            kz_copy(1, s, above).wait_recv()

            @pl.when(zl > 0)
            def _():
                kz_copy(1, s + 1, above).start()

        @pl.when(below >= 0)
        def _():
            x_send(below)

        @pl.when(above < NL)
        def _():
            x_send(above)

        @pl.when(below >= 0)
        def _():
            stats(x * NL + below, 1)

        for way, part in ((0, 0), (1, 1), (0, 1), (1, 0)):
            most = NL if way == part else NL - 1

            @pl.when((s >= 1) & (s <= most))
            def _():
                ring(way, part, s - 1, "wait_recv")

                @pl.when(s < most)
                def _():
                    ring(way, part, s, "start")

        @pl.when(s == 1)
        def _():
            x_pass(zl)

        @pl.when(s >= 2)
        def _():
            x_pass(zl + 1 - s)
            x_pass(zl - 1 + s)

        @pl.when(s >= 5)
        def _():
            pack_rows(0, s - 5)

            launch_rows(0, s - 5)

    @pl.when(x == 0)
    def _():
        @pl.loop(0, 4)
        def _(n):
            pack_rows(1, n)
            launch_rows(1, n)

    @pl.when(x >= 2)
    def _():
        @pl.loop(0, NL)
        def _(j):
            xh_copy(x - 2, j).wait_recv()
            xt_copy(x - 2, j).wait_recv()

        @pl.loop(0, 2)
        def _(i):
            stats((x - 2) * NL + i * 4, 4)

    stat[2:3, :] = stat[2:3, :] / stat[1:2, :]
    stat[0:1, :] = stat[0:1, :] + jnp.log2(stat[1:2, :])
    dqt[...] = jnp.zeros_like(dqt)
    def span(part):
        return pl.ds(pl.multiple_of(part * CHUNK, CHUNK), CHUNK)

    def grads(g, part, masked=False):
        first = (zl - part * 2) * TOK if masked else None
        keys, s, dp = scores(g * NL + part * 2, 2, first)
        p = jnp.exp2(s - stat[0:1, :])
        ds = (p * (dp - stat[2:3, :])).astype(BF16)
        dkv[g, span(part), HEAD_DIM:] = dot_nn(p.astype(BF16), dos[...])
        dkv[g, span(part), :HEAD_DIM] = dot_nn(ds, qs[...])
        dqt[...] += dot_tn(keys, ds)

    def r1_copy(way, part):
        return remote(
            xs1.at[part], xr1.at[part], (r1_s.at[part], r1_r.at[part]), (x_up, x_down)[way]
        )

    def r2_copy(way, part, src=None):
        ref = xs2.at[way, part] if src is None else src
        return remote(
            ref, xr2.at[way, part], (r2_s.at[way, part], r2_r.at[way, part]), (x_up, x_down)[way]
        )

    def rz_send(j):
        return remote(zs.at[j], zr.at[zl], (rz_s.at[j], rz_r.at[zl]), line_dev(j))

    def rz_got(j):
        return remote(zs.at[j], zr.at[j], (rz_s.at[j], rz_r.at[j]), line_dev(j))

    def z_spread(part):
        @pl.loop(0, 2)
        def _(i):
            j = part * 2 + (zl + i) % 2

            @pl.when(j != zl)
            def _():
                zs[j] = dkv[x, pl.ds(pl.multiple_of(j * TOK, TOK), TOK), :].astype(BF16)
                rz_send(j).start()

    @pl.when(x >= 2)
    def _():
        @pl.loop(0, 4)
        def _(part):
            grads(x - 2, part)
            xs1[part] = dkv[x - 2, span(part), :].astype(BF16)
            pl.when(part < 2)(lambda: r1_copy(0, part).start())
            pl.when(part >= 2)(lambda: r1_copy(1, part).start())

    @pl.when(x == 3)
    def _():
        @pl.loop(0, 4)
        def _(n):
            part = (n + 2) % 4
            grads(0, part)

            @pl.when(part < 2)
            def _():
                r1_copy(0, part).wait_recv()
                dkv[0, span(part), :] += xr1[part].astype(F32)

            xs2[0, part] = dkv[0, span(part), :].astype(BF16)
            r2_copy(0, part).start()

    @pl.when(x >= 1)
    def _():
        @pl.loop(0, 4)
        def _(part):
            grads(x - 1, part)

            @pl.when((part >= 2) & (x < 3))
            def _():
                r1_copy(1, part).wait_recv()
                dkv[x - 1, span(part), :] += xr1[part].astype(F32)

            xs2[1, part] = dkv[x - 1, span(part), :].astype(BF16)
            r2_copy(1, part).start()

    @pl.loop(0, 4)
    def _(part):
        grads(x, part, True)
        pl.when(x == 3)(lambda: z_spread(part))

    @pl.when(x >= 1)
    def _():
        @pl.loop(0, 4)
        def _(n):
            pack_rows(1, n)
            launch_rows(1, n)

    @pl.when(x == 0)
    def _():
        @pl.loop(0, 2)
        def _(part):
            r1_copy(0, part).wait_recv()
            r2_copy(0, part, xr1.at[part]).start()

    for h in range(GROUP):
        at_head = slice(h * TOK, (h + 1) * TOK)
        dq_ref[:, at_head] = (dqt[:, at_head].T * SCALE).astype(BF16)

    def all_copy(side):
        ref = rcv.at[side, 0]
        return remote(ref, ref, (all_s, all_r), twin)

    def core_copy(side, d):
        ref = rcv.at[side, 1, d]
        return remote(ref, ref, (core_s.at[d], core_r.at[d]), twin)

    @pl.loop(1, 16)
    def _(i):
        a2a_in(0, (plane + 16 - i) % 16).wait_recv()

    all_copy(core).start()

    @pl.loop(0, 4)
    def _(part):
        @pl.when(x <= 2)
        def _():
            r2_copy(1, part).wait_recv()
            dkv[x, span(part), :] += xr2[1, part].astype(F32)

            @pl.when((x == 0) | ((x == 1) & (part < 2)))
            def _():
                r2_copy(0, part).wait_recv()
                dkv[x, span(part), :] += xr2[0, part].astype(F32)

            z_spread(part)

    core_copy(core, plane).start()

    @pl.loop(1, 16)
    def _(i):
        d = (plane + 16 - i) % 16
        a2a_in(1, d).wait_recv()
        core_copy(core, d).start()

    all_copy(1 - core).wait_recv()

    @pl.loop(0, 16)
    def _(i):
        core_copy(1 - core, (plane + 16 - i) % 16).wait_recv()

    block = lax.broadcasted_iota(jnp.int32, (4 * PACK, PART), 0) % NL
    low = (z + 12 + (block + 12 - zl) % NL) % NZ < NL

    @pl.loop(0, 4)
    def _(i):
        total = jnp.zeros((4 * PACK, w_ref.shape[0]), F32)
        for side in range(2):
            near = rcv[side, 0, pl.ds(i * 4, 4)].reshape(4 * PACK, PART)
            far = rcv[side, 1, pl.ds(i * 4, 4)].reshape(4 * PACK, PART)
            for part in range(2):
                left = jnp.where(low, near, far) if part == 0 else jnp.where(low, far, near)
                begin = (part * 2 + side) * PART
                total += dot_nt(left, w_ref[:, begin : begin + PART])
        for n in range(SLOTS):
            parts = [total[m * PACK + n * NL : m * PACK + (n + 1) * NL, :] for m in range(4)]
            here = pl.ds(pl.multiple_of(i * 4 * NL, 4 * NL), 4 * NL)
            hid_ref[n, here, :] = jnp.concatenate(parts, axis=0).astype(BF16)

    mine = pl.ds(pl.multiple_of(zl * TOK, TOK), TOK)

    @pl.loop(1, NL)
    def _(i):
        j = (zl + i) % NL
        rz_got(j).wait_recv()
        dkv[x, mine, :] += zr[j].astype(F32)

    own = dkv[x, mine, :]
    dk_ref[...] = (own[:, :HEAD_DIM] * SCALE).astype(BF16)
    dv_ref[...] = own[:, HEAD_DIM:].astype(BF16)

    @pl.loop(0, NL)
    def _(s):
        @pl.when((zl < NL - 1) & (zl - s >= 0))
        def _():
            kz_copy(0, s, zl - s).wait_send()

        @pl.when((zl > 0) & (zl + s < NL))
        def _():
            kz_copy(1, s, zl + s).wait_send()

        ring(0, 0, s, "wait_send")
        ring(1, 1, s, "wait_send")

        @pl.when(s < NL - 1)
        def _():
            ring(0, 1, s, "wait_send")
            ring(1, 0, s, "wait_send")

        @pl.when(x <= 2)
        def _():
            xf_copy(x, s).wait_send()

        @pl.when(x == 0)
        def _():
            xb_copy(0, x, s).wait_send()

        @pl.when(x <= 1)
        def _():
            xb_copy(1, x, s).wait_send()

        @pl.when((x == 1) | (x == 2))
        def _():
            xh_copy(x - 1, s).wait_send()

        @pl.when((x == 3) | (x == 0))
        def _():
            xt_copy((x + 1) % NX, s).wait_send()

    all_copy(core).wait_send()
    core_copy(core, plane).wait_send()

    @pl.loop(0, 15)
    def _(r):
        a2a_out(0, r).wait_send()
        a2a_out(1, r).wait_send()
        core_copy(core, (plane + r + 1) % 16).wait_send()

    @pl.loop(0, 4)
    def _(part):
        @pl.when(x >= 2)
        def _():
            pl.when(part < 2)(lambda: r1_copy(0, part).wait_send())
            pl.when(part >= 2)(lambda: r1_copy(1, part).wait_send())

        @pl.when(x >= 1)
        def _():
            r2_copy(1, part).wait_send()

        @pl.when((x == 3) | ((x == 0) & (part < 2)))
        def _():
            r2_copy(0, part).wait_send()

    @pl.loop(1, NL)
    def _(i):
        rz_send((zl + i) % NL).wait_send()


def per_device(queries, keys, values, out_grad, mixed_grad, expert_ids, combine, w_down):
    vmem = pl.BlockSpec(memory_space=pltpu.VMEM)
    dma = pltpu.SemaphoreType.DMA
    hid = w_down.shape[1]
    shapes = (
        jax.ShapeDtypeStruct((TOK, ROWS), BF16),
        jax.ShapeDtypeStruct((TOK, HEAD_DIM), BF16),
        jax.ShapeDtypeStruct((TOK, HEAD_DIM), BF16),
        jax.ShapeDtypeStruct((SLOTS, EXPERTS, hid), BF16),
    )
    scratch = [
        pltpu.VMEM((NX * NL, TOK, WIDE), BF16),
        pltpu.VMEM((NZ, SIDE + TOK, PART), BF16),
        pltpu.VMEM((16, PACK, RUN), BF16),
        pltpu.VMEM((2, 16, PACK, PART), BF16),
        pltpu.VMEM((2, 2, 16, PACK, PART), BF16),
        pltpu.VMEM((ROWS, HEAD_DIM), BF16),
        pltpu.VMEM((ROWS, HEAD_DIM), BF16),
        pltpu.VMEM((8, ROWS), F32),
        pltpu.VMEM((HEAD_DIM, ROWS), F32),
        pltpu.VMEM((NX, RUN, WIDE), F32),
        pltpu.VMEM((4, CHUNK, WIDE), BF16),
        pltpu.VMEM((4, CHUNK, WIDE), BF16),
        pltpu.VMEM((2, 4, CHUNK, WIDE), BF16),
        pltpu.VMEM((2, 4, CHUNK, WIDE), BF16),
        pltpu.VMEM((NL, TOK, WIDE), BF16),
        pltpu.VMEM((NL, TOK, WIDE), BF16),
    ]
    for shape in (
        (2, 2, NL), (2, NL), (NL,), (NL,), (2, NL), (NL,),
        (2, 16), (), (16,), (4,), (2, 4), (NL,),
    ):
        scratch += [dma(shape), dma(shape)]
    dq, dk, dv, hidden = pl.pallas_call(
        kernel,
        out_shape=shapes,
        in_specs=[vmem] * 8,
        out_specs=(vmem,) * 4,
        scratch_shapes=scratch,
        compiler_params=pltpu.CompilerParams(
            collective_id=0, has_side_effects=True, vmem_limit_bytes=56 * 1024 * 1024
        ),
        name="layer_backward",
    )(queries[0], out_grad[0], keys[0], values[0], mixed_grad, expert_ids.T, combine.T, w_down[0])
    return dq[None], dk[None], dv[None], hidden.transpose(1, 0, 2)[None]


def solution(mesh):
    placed = (
        P("dp", "ctx", "tp"),
        P("dp", "ctx", "tp"),
        P("dp", "ctx", "tp"),
        P("dp", "ctx", "tp"),
        P(("dp", "ctx"), "tp"),
        P(("dp", "ctx"), None),
        P(("dp", "ctx"), None),
        P(("dp", "ctx"), "tp", None),
    )
    return jax.shard_map(
        per_device,
        mesh=mesh,
        in_specs=placed,
        out_specs=(
            P("dp", "ctx", "tp"),
            P("dp", "ctx", "tp"),
            P("dp", "ctx", "tp"),
            P(("dp", "ctx"), None, None, "tp"),
        ),
        check_vma=False,
    )
```

time: 130 us -> 113 us (0.87)
  the two profiles are of different devices: /device:TPU:60 before, /device:TPU:1 now
where the time goes in v2:
time: 113 us; the launch traced here: 112 us
  Pallas kernels  105 us (93%)
  local copies, waits for them, and re-layouts  6.66 us (6%)
    pallas_call x1, Pallas kernels, per_device(): pl.pallas_call(kernel, out_shape=shapes, in_specs=[vmem] * 8, out_specs=(...  105 us
    unnamed x4, local copies, waits for them, and re-layouts  6.66 us

profile of v2, /device:TPU:1, one launch (start us, length us, event | category | flops | bytes accessed | tf_op | source)
XLA Modules:
  0.0 112.4 jit_solution(9794529902219058236)
XLA Ops:
  0.6 105.1 %layer_backward.1 = (bf16[128,1024]{1,0:T(8,128)(2,1)}, bf16[128,128]{1,0:T(8,128)(2,1)}, bf16[128,128]{1,0:T(8,128)(2,1)}, bf16[10,128,384]{2,1,0:T(8,128)(2,1)}) custom-call(bf16[128,1024]{1,0:T(8,128)(2,1)} %bitcast.16, bf16[128,1024]{1,0:T(8,128)(2,1)} %bitcast.17, bf16[128,128]{1,0:T(8,128)(2,1)} %bitcast.20, bf16[128,128]{1,0:T(8,128)(2,1)} %bitcast.21, ...), custom_call_target="tpu_custom_call" | custom-call | tf_op jit(solution)/shard_map/layer_backward/pallas_call | solution.py:661
  105.7 1.7 %copy.16 = bf16[1,128,1024]{2,1,0:T(8,128)(2,1)} copy(bf16[1,128,1024]{2,1,0:T(8,128)(2,1)} %bitcast.15) | data formatting | bytes 524288
  107.4 1.4 %copy.17 = bf16[1,128,128]{2,1,0:T(8,128)(2,1)} copy(bf16[1,128,128]{2,1,0:T(8,128)(2,1)} %bitcast.19) | data formatting | bytes 65536
  108.8 1.4 %copy.18 = bf16[1,128,128]{2,1,0:T(8,128)(2,1)} copy(bf16[1,128,128]{2,1,0:T(8,128)(2,1)} %bitcast.18) | data formatting | bytes 65536
  110.1 2.2 %copy.19 = bf16[1,128,10,384]{3,1,2,0:T(8,128)(2,1)} copy(bf16[1,128,10,384]{3,1,2,0:T(8,128)(2,1)} %bitcast.14) | data formatting | bytes 1966080

commit v3 on v2

--- a/solution.py
+++ b/solution.py
@@ -17,11 +17,14 @@
 NX, NY, NL, NZ = 4, 4, 8, 16
 RUN = NL * TOK
 WIDE = 2 * HEAD_DIM
-CHUNK = 256
+PARTS = 4
+SLICE = TOK // PARTS
+CHUNK = RUN // PARTS
 ROWS = GROUP * TOK
 PACK = NL * SLOTS
 SIDE = 16
 PART = 512
+FEW = 4 * SLOTS
 SCALE = HEAD_DIM**-0.5
 SCALE2 = SCALE / math.log(2.0)
 MASKED = -1e30
@@ -72,7 +75,7 @@
 def kernel(
     q_ref, do_ref, k_ref, v_ref, mg_ref, ids_ref, comb_ref, w_ref,
     dq_ref, dk_ref, dv_ref, hid_ref,
-    kv, rows, picks, snd, rcv, qs, dos, stat, dqt, dkv, xs1, xr1, xs2, xr2, zs, zr,
+    kv, rows, picks, snd, rcv, sums, qs, dos, stat, dqt, dkv, xs1, xr1, xs2, xr2, zs, zr,
     ring_s, ring_r, kz_s, kz_r, xf_s, xf_r, xh_s, xh_r, xb_s, xb_r, xt_s, xt_r,
     a2a_s, a2a_r, all_s, all_r, core_s, core_r, r1_s, r1_r, r2_s, r2_r, rz_s, rz_r,
 ):
@@ -236,24 +239,32 @@
                 stats(j, 1)
 
     pick_row = lax.broadcasted_iota(jnp.int32, (16, TOK), 0)
-    pick_block = lax.broadcasted_iota(jnp.int32, (NL, TOK), 0)
-
-    def make_pick(r):
+    pick_sub = lax.broadcasted_iota(jnp.int32, (8, TOK), 0)
+
+    def window(w):
+        first = jnp.where(w == 0, 6, jnp.where(w == 1, 4, jnp.where(w == 2, 12, 14)))
+        return first, (first + jnp.where(w == 0, 2, jnp.where(w == 3, 2, 6))) % NZ
+
+    def make_pick(w, r):
         d = (plane + r + 1) % 16
         expert = (d // NX) * (NX * NL) + (d % NX) * NL + zl
         key = jnp.where(pick_row < SLOTS, expert * SLOTS + pick_row, -1).astype(F32)
+        start = window(w)
         columns = []
-        for n in range(NL):
-            named = rows[4 + n, pl.ds(0, SIDE), :].astype(F32)
+        for j in range(4):
+            named = rows[start[j // 2] + j % 2, pl.ds(0, SIDE), :].astype(F32)
             target = named[:8, :TOK] * float(SLOTS) + named[:8, TOK : 2 * TOK]
             weight = named[:8, 2 * TOK : 3 * TOK]
-            window = jnp.zeros((16, TOK), F32)
+            chosen = jnp.zeros((16, TOK), F32)
             for k in range(8):
-                window += jnp.where(target[k : k + 1, :] == key, weight[k : k + 1, :], 0.0)
-            mine = pick_block == (zl + 4 + n) % NL
-            column = [jnp.where(mine, window[i : i + 1, :], 0.0) for i in range(SLOTS)]
-            columns.append(jnp.concatenate(column, axis=0).astype(BF16))
-        picks[r] = jnp.concatenate(columns, axis=1)
+                chosen += jnp.where(target[k : k + 1, :] == key, weight[k : k + 1, :], 0.0)
+            column = [
+                jnp.where(pick_sub == j, chosen[i : i + 1, :], 0.0)
+                + jnp.where(pick_sub == 4 + j, chosen[i + 1 : i + 2, :], 0.0)
+                for i in range(0, SLOTS, 2)
+            ]
+            columns.append(jnp.concatenate(column, axis=0))
+        picks[w, r] = jnp.concatenate(columns, axis=1)
 
     def a2a_out(w, r):
         return remote(
@@ -267,30 +278,33 @@
         )
 
     def pack_rows(w, n):
-        if w == 0:
-            @pl.loop(0, 4)
+        @pl.when(w < 2)
+        def _():
+            @pl.loop(0, 8)
             def _(i):
-                make_pick(n * 4 + i)
-
-        total = jnp.zeros((4 * PACK, PART), F32)
-        for m, start in enumerate(((4, 8), (12, 0))[w]):
-            source = rows[start : start + 4, SIDE:, :].reshape(4 * TOK, PART)
-            chosen = picks[pl.ds(n * 4, 4), :, m * 4 * TOK : (m + 1) * 4 * TOK]
-            total += dot_nn(chosen.reshape(4 * PACK, 4 * TOK), source)
-        snd[w, pl.ds(n * 4, 4)] = total.astype(BF16).reshape(4, PACK, PART)
-
-        @pl.when(n == 3)
+                make_pick(w, n * 8 + i)
+
+        group = jnp.where(w < 2, w, 3 - w)
+        total = jnp.zeros((8 * FEW, PART), F32)
+        for m, start in enumerate(window(w)):
+            source = rows[pl.ds(start, 2), SIDE:, :].reshape(2 * TOK, PART)
+            chosen = picks[group, pl.ds(n * 8, 8), :, m * 2 * TOK : (m + 1) * 2 * TOK]
+            total += dot_nn(chosen.reshape(8 * FEW, 2 * TOK).astype(BF16), source)
+        for i in range(8):
+            mine = total[i * FEW : (i + 1) * FEW]
+            mine = jnp.concatenate([mine[:, : PART // 2], mine[:, PART // 2 :]], axis=0)
+            snd[w, n * 8 + i] = mine.astype(BF16)
+
+        @pl.when(n == 1)
         def _():
             rcv[core, w, plane] = snd[w, 15]
 
     def launch_rows(w, n):
-        @pl.loop(0, 4)
+        @pl.loop(0, 8)
         def _(i):
-            r = n * 4 + i
-
-            @pl.when(r < 15)
-            def _():
-                a2a_out(w, r).start()
+            @pl.when(n * 8 + i < 15)
+            def _():
+                a2a_out(w, n * 8 + i).start()
 
     @pl.when(zl < NL - 1)
     def _():
@@ -354,23 +368,29 @@
         def _():
             x_pass(zl)
 
-        @pl.when(s >= 2)
-        def _():
-            x_pass(zl + 1 - s)
-            x_pass(zl - 1 + s)
-
-        @pl.when(s >= 5)
-        def _():
-            pack_rows(0, s - 5)
-
-            launch_rows(0, s - 5)
+        @pl.when(s >= 1)
+        def _():
+            x_pass(zl - s)
+            x_pass(zl + s)
+
+        @pl.when((s >= 2) & (s < NL))
+        def _():
+            pack_rows((s - 2) // 2, s % 2)
+
+        @pl.when((s >= 2) & (s < 6))
+        def _():
+            launch_rows((s - 2) // 2, s % 2)
+
+    @pl.loop(0, 2)
+    def _(n):
+        launch_rows(2, n)
 
     @pl.when(x == 0)
     def _():
-        @pl.loop(0, 4)
+        @pl.loop(0, 2)
         def _(n):
-            pack_rows(1, n)
-            launch_rows(1, n)
+            pack_rows(3, n)
+            launch_rows(3, n)
 
     @pl.when(x >= 2)
     def _():
@@ -386,16 +406,20 @@
     stat[2:3, :] = stat[2:3, :] / stat[1:2, :]
     stat[0:1, :] = stat[0:1, :] + jnp.log2(stat[1:2, :])
     dqt[...] = jnp.zeros_like(dqt)
-    def span(part):
-        return pl.ds(pl.multiple_of(part * CHUNK, CHUNK), CHUNK)
-
     def grads(g, part, masked=False):
-        first = (zl - part * 2) * TOK if masked else None
-        keys, s, dp = scores(g * NL + part * 2, 2, first)
+        here = pl.ds(pl.multiple_of(part * SLICE, SLICE), SLICE)
+        block = kv[pl.ds(g * NL, NL), here, :].reshape(CHUNK, WIDE)
+        keys, values = block[:, :HEAD_DIM], block[:, HEAD_DIM:]
+        s = dot_nt(keys, qs[...]) * SCALE2
+        if masked:
+            row = lax.broadcasted_iota(jnp.int32, (CHUNK, ROWS), 0)
+            place = row // SLICE * TOK + row % SLICE
+            s = jnp.where(place <= lane + (zl * TOK - part * SLICE), s, MASKED)
+        dp = dot_nt(values, dos[...])
         p = jnp.exp2(s - stat[0:1, :])
         ds = (p * (dp - stat[2:3, :])).astype(BF16)
-        dkv[g, span(part), HEAD_DIM:] = dot_nn(p.astype(BF16), dos[...])
-        dkv[g, span(part), :HEAD_DIM] = dot_nn(ds, qs[...])
+        dkv[g, part, :, HEAD_DIM:] = dot_nn(p.astype(BF16), dos[...])
+        dkv[g, part, :, :HEAD_DIM] = dot_nn(ds, qs[...])
         dqt[...] += dot_tn(keys, ds)
 
     def r1_copy(way, part):
@@ -409,28 +433,29 @@
             ref, xr2.at[way, part], (r2_s.at[way, part], r2_r.at[way, part]), (x_up, x_down)[way]
         )
 
-    def rz_send(j):
-        return remote(zs.at[j], zr.at[zl], (rz_s.at[j], rz_r.at[zl]), line_dev(j))
-
-    def rz_got(j):
-        return remote(zs.at[j], zr.at[j], (rz_s.at[j], rz_r.at[j]), line_dev(j))
+    def rz_send(part, j):
+        return remote(
+            zs.at[part, j], zr.at[part, zl], (rz_s.at[part, j], rz_r.at[part, zl]), line_dev(j)
+        )
+
+    def rz_got(part, j):
+        return remote(
+            zs.at[part, j], zr.at[part, j], (rz_s.at[part, j], rz_r.at[part, j]), line_dev(j)
+        )
 
     def z_spread(part):
-        @pl.loop(0, 2)
+        zs[part] = dkv[x, part].astype(BF16).reshape(NL, SLICE, WIDE)
+
+        @pl.loop(1, NL)
         def _(i):
-            j = part * 2 + (zl + i) % 2
-
-            @pl.when(j != zl)
-            def _():
-                zs[j] = dkv[x, pl.ds(pl.multiple_of(j * TOK, TOK), TOK), :].astype(BF16)
-                rz_send(j).start()
+            rz_send(part, (zl + i) % NL).start()
 
     @pl.when(x >= 2)
     def _():
         @pl.loop(0, 4)
         def _(part):
             grads(x - 2, part)
-            xs1[part] = dkv[x - 2, span(part), :].astype(BF16)
+            xs1[part] = dkv[x - 2, part].astype(BF16)
             pl.when(part < 2)(lambda: r1_copy(0, part).start())
             pl.when(part >= 2)(lambda: r1_copy(1, part).start())
 
@@ -444,9 +469,9 @@
             @pl.when(part < 2)
             def _():
                 r1_copy(0, part).wait_recv()
-                dkv[0, span(part), :] += xr1[part].astype(F32)
-
-            xs2[0, part] = dkv[0, span(part), :].astype(BF16)
+                dkv[0, part] += xr1[part].astype(F32)
+
+            xs2[0, part] = dkv[0, part].astype(BF16)
             r2_copy(0, part).start()
 
     @pl.when(x >= 1)
@@ -458,9 +483,9 @@
             @pl.when((part >= 2) & (x < 3))
             def _():
                 r1_copy(1, part).wait_recv()
-                dkv[x - 1, span(part), :] += xr1[part].astype(F32)
-
-            xs2[1, part] = dkv[x - 1, span(part), :].astype(BF16)
+                dkv[x - 1, part] += xr1[part].astype(F32)
+
+            xs2[1, part] = dkv[x - 1, part].astype(BF16)
             r2_copy(1, part).start()
 
     @pl.loop(0, 4)
@@ -470,10 +495,10 @@
 
     @pl.when(x >= 1)
     def _():
-        @pl.loop(0, 4)
+        @pl.loop(0, 2)
         def _(n):
-            pack_rows(1, n)
-            launch_rows(1, n)
+            pack_rows(3, n)
+            launch_rows(3, n)
 
     @pl.when(x == 0)
     def _():
@@ -486,77 +511,111 @@
         at_head = slice(h * TOK, (h + 1) * TOK)
         dq_ref[:, at_head] = (dqt[:, at_head].T * SCALE).astype(BF16)
 
-    def all_copy(side):
-        ref = rcv.at[side, 0]
-        return remote(ref, ref, (all_s, all_r), twin)
+    def all_copy(side, w):
+        ref = rcv.at[side, w]
+        return remote(ref, ref, (all_s.at[w], all_r.at[w]), twin)
+
+    row = lax.broadcasted_iota(jnp.int32, (8 * PACK, PART // 2), 0) % 4
+    spot = row + jnp.where(row < 2, 4, 8)
+    low = ((z + 14 + row) % NZ < NL, (z + 8 + spot) % NZ < NL)
+
+    def expert_group(group):
+        @pl.loop(0, 2)
+        def _(i):
+            total = jnp.zeros((8 * FEW, w_ref.shape[0]), F32)
+            for side in range(2):
+                near = rcv[side, group, pl.ds(i * 8, 8)].reshape(8 * PACK, PART // 2)
+                far = rcv[side, 3 - group, pl.ds(i * 8, 8)].reshape(8 * PACK, PART // 2)
+                for part in range(2):
+                    a, b = (near, far) if part == 0 else (far, near)
+                    left = jnp.where(low[group], a, b).astype(F32)
+                    for m in range(2):
+                        begin = (part * 2 + side) * PART + m * (PART // 2)
+                        cuts = [
+                            left[n * PACK + m * FEW : n * PACK + (m + 1) * FEW] for n in range(8)
+                        ]
+                        total += dot_nt(
+                            jnp.concatenate(cuts, axis=0).astype(BF16),
+                            w_ref[:, begin : begin + PART // 2],
+                        )
+            sums[group, pl.ds(pl.multiple_of(i * 8 * FEW, 8), 8 * FEW), :] = total
 
     def core_copy(side, d):
-        ref = rcv.at[side, 1, d]
+        ref = rcv.at[side, 3, d]
         return remote(ref, ref, (core_s.at[d], core_r.at[d]), twin)
 
-    @pl.loop(1, 16)
-    def _(i):
-        a2a_in(0, (plane + 16 - i) % 16).wait_recv()
-
-    all_copy(core).start()
+    def swap_rows(w):
+        @pl.loop(1, 16)
+        def _(i):
+            a2a_in(w, (plane + 16 - i) % 16).wait_recv()
+
+        all_copy(core, w).start()
+
+    pl.loop(0, 3)(swap_rows)
 
     @pl.loop(0, 4)
     def _(part):
         @pl.when(x <= 2)
         def _():
             r2_copy(1, part).wait_recv()
-            dkv[x, span(part), :] += xr2[1, part].astype(F32)
+            dkv[x, part] += xr2[1, part].astype(F32)
 
             @pl.when((x == 0) | ((x == 1) & (part < 2)))
             def _():
                 r2_copy(0, part).wait_recv()
-                dkv[x, span(part), :] += xr2[0, part].astype(F32)
+                dkv[x, part] += xr2[0, part].astype(F32)
 
             z_spread(part)
 
+    @pl.loop(1, 3)
+    def _(w):
+        all_copy(1 - core, w).wait_recv()
+
+    expert_group(1)
     core_copy(core, plane).start()
 
     @pl.loop(1, 16)
     def _(i):
         d = (plane + 16 - i) % 16
-        a2a_in(1, d).wait_recv()
+        a2a_in(3, d).wait_recv()
         core_copy(core, d).start()
-
-    all_copy(1 - core).wait_recv()
 
     @pl.loop(0, 16)
     def _(i):
         core_copy(1 - core, (plane + 16 - i) % 16).wait_recv()
 
-    block = lax.broadcasted_iota(jnp.int32, (4 * PACK, PART), 0) % NL
-    low = (z + 12 + (block + 12 - zl) % NL) % NZ < NL
+    all_copy(1 - core, 0).wait_recv()
+    expert_group(0)
+
+    goal = lax.broadcasted_iota(jnp.int32, (PACK, PACK), 0)
+    have = lax.broadcasted_iota(jnp.int32, (PACK, PACK), 1)
+    have_row = have % 4
+    have_spot = jnp.where(have < FEW, have_row + 6, have_row + jnp.where(have_row < 2, 4, 8))
+    fits = (goal // NL == have % FEW // 4) & (goal % NL == (zl + have_spot) % NL)
+    order = jnp.where(fits, 1.0, 0.0).astype(BF16)
 
     @pl.loop(0, 4)
     def _(i):
-        total = jnp.zeros((4 * PACK, w_ref.shape[0]), F32)
-        for side in range(2):
-            near = rcv[side, 0, pl.ds(i * 4, 4)].reshape(4 * PACK, PART)
-            far = rcv[side, 1, pl.ds(i * 4, 4)].reshape(4 * PACK, PART)
-            for part in range(2):
-                left = jnp.where(low, near, far) if part == 0 else jnp.where(low, far, near)
-                begin = (part * 2 + side) * PART
-                total += dot_nt(left, w_ref[:, begin : begin + PART])
+        outs = []
+        for n in range(4):
+            at_rows = pl.ds(pl.multiple_of((i * 4 + n) * FEW, 8), FEW)
+            both = [sums[0, at_rows, :], sums[1, at_rows, :]]
+            outs.append(dot_nn(order, jnp.concatenate(both, axis=0).astype(BF16)))
         for n in range(SLOTS):
-            parts = [total[m * PACK + n * NL : m * PACK + (n + 1) * NL, :] for m in range(4)]
+            parts = [out[n * NL : (n + 1) * NL, :] for out in outs]
             here = pl.ds(pl.multiple_of(i * 4 * NL, 4 * NL), 4 * NL)
             hid_ref[n, here, :] = jnp.concatenate(parts, axis=0).astype(BF16)
 
-    mine = pl.ds(pl.multiple_of(zl * TOK, TOK), TOK)
-
-    @pl.loop(1, NL)
-    def _(i):
-        j = (zl + i) % NL
-        rz_got(j).wait_recv()
-        dkv[x, mine, :] += zr[j].astype(F32)
-
-    own = dkv[x, mine, :]
-    dk_ref[...] = (own[:, :HEAD_DIM] * SCALE).astype(BF16)
-    dv_ref[...] = own[:, HEAD_DIM:].astype(BF16)
+    @pl.loop(0, PARTS)
+    def _(part):
+        own = dkv[x, part, pl.ds(pl.multiple_of(zl * SLICE, SLICE), SLICE), :]
+        for i in range(1, NL):
+            j = (zl + i) % NL
+            rz_got(part, j).wait_recv()
+            own += zr[part, j].astype(F32)
+        here = pl.ds(pl.multiple_of(part * SLICE, SLICE), SLICE)
+        dk_ref[here, :] = (own[:, :HEAD_DIM] * SCALE).astype(BF16)
+        dv_ref[here, :] = own[:, HEAD_DIM:].astype(BF16)
 
     @pl.loop(0, NL)
     def _(s):
@@ -596,13 +655,16 @@
         def _():
             xt_copy((x + 1) % NX, s).wait_send()
 
-    all_copy(core).wait_send()
+    @pl.loop(0, 3)
+    def _(w):
+        all_copy(core, w).wait_send()
+
     core_copy(core, plane).wait_send()
 
     @pl.loop(0, 15)
     def _(r):
-        a2a_out(0, r).wait_send()
-        a2a_out(1, r).wait_send()
+        for w in range(4):
+            a2a_out(w, r).wait_send()
         core_copy(core, (plane + r + 1) % 16).wait_send()
 
     @pl.loop(0, 4)
@@ -622,7 +684,13 @@
 
     @pl.loop(1, NL)
     def _(i):
-        rz_send((zl + i) % NL).wait_send()
+        for part in range(PARTS):
+            rz_send(part, (zl + i) % NL).wait_send()
+
+
+def place(*refs):
+    for source, target in zip(refs[:4], refs[4:]):
+        target[...] = source[...]
 
 
 def per_device(queries, keys, values, out_grad, mixed_grad, expert_ids, combine, w_down):
@@ -638,24 +706,25 @@
     scratch = [
         pltpu.VMEM((NX * NL, TOK, WIDE), BF16),
         pltpu.VMEM((NZ, SIDE + TOK, PART), BF16),
-        pltpu.VMEM((16, PACK, RUN), BF16),
-        pltpu.VMEM((2, 16, PACK, PART), BF16),
-        pltpu.VMEM((2, 2, 16, PACK, PART), BF16),
+        pltpu.VMEM((2, 16, FEW, PART), F32),
+        pltpu.VMEM((4, 16, PACK, PART // 2), BF16),
+        pltpu.VMEM((2, 4, 16, PACK, PART // 2), BF16),
+        pltpu.VMEM((2, 16 * FEW, hid), F32),
         pltpu.VMEM((ROWS, HEAD_DIM), BF16),
         pltpu.VMEM((ROWS, HEAD_DIM), BF16),
         pltpu.VMEM((8, ROWS), F32),
         pltpu.VMEM((HEAD_DIM, ROWS), F32),
-        pltpu.VMEM((NX, RUN, WIDE), F32),
+        pltpu.VMEM((NX, PARTS, CHUNK, WIDE), F32),
         pltpu.VMEM((4, CHUNK, WIDE), BF16),
         pltpu.VMEM((4, CHUNK, WIDE), BF16),
         pltpu.VMEM((2, 4, CHUNK, WIDE), BF16),
         pltpu.VMEM((2, 4, CHUNK, WIDE), BF16),
-        pltpu.VMEM((NL, TOK, WIDE), BF16),
-        pltpu.VMEM((NL, TOK, WIDE), BF16),
+        pltpu.VMEM((PARTS, NL, SLICE, WIDE), BF16),
+        pltpu.VMEM((PARTS, NL, SLICE, WIDE), BF16),
     ]
     for shape in (
         (2, 2, NL), (2, NL), (NL,), (NL,), (2, NL), (NL,),
-        (2, 16), (), (16,), (4,), (2, 4), (NL,),
+        (4, 16), (3,), (16,), (4,), (2, 4), (PARTS, NL),
     ):
         scratch += [dma(shape), dma(shape)]
     dq, dk, dv, hidden = pl.pallas_call(
@@ -669,6 +738,13 @@
         ),
         name="layer_backward",
     )(queries[0], out_grad[0], keys[0], values[0], mixed_grad, expert_ids.T, combine.T, w_down[0])
+    dq, dk, dv, hidden = pl.pallas_call(
+        place,
+        out_shape=shapes,
+        in_specs=[vmem] * 4,
+        out_specs=(vmem,) * 4,
+        name="place_outputs",
+    )(dq, dk, dv, hidden)
     return dq[None], dk[None], dv[None], hidden.transpose(1, 0, 2)[None]
 
 

time: 113 us -> 104 us (0.920)
  the two profiles are of different devices: /device:TPU:1 before, /device:TPU:8 now
where the time goes in v3:
time: 104 us
  Pallas kernels  103 us (99%)
    pallas_call x1, Pallas kernels, per_device(): pl.pallas_call(kernel, out_shape=shapes, in_specs=[vmem] * 8, out_specs=(...  101 us
    pallas_call x1, Pallas kernels, per_device(): pl.pallas_call(place, out_shape=shapes, in_specs=[vmem] * 4, out_specs=(v...  2.39 us

profile of v3, /device:TPU:8, one launch (start us, length us, event | category | flops | bytes accessed | tf_op | source)
XLA Modules:
  0.0 103.8 jit_solution(16707515159311114785)
XLA Ops:
  0.6 100.7 %layer_backward.1 = (bf16[128,1024]{1,0:T(8,128)(2,1)}, bf16[128,128]{1,0:T(8,128)(2,1)}, bf16[128,128]{1,0:T(8,128)(2,1)}, bf16[10,128,384]{2,1,0:T(8,128)(2,1)}) custom-call(bf16[128,1024]{1,0:T(8,128)(2,1)} %bitcast.14, bf16[128,1024]{1,0:T(8,128)(2,1)} %bitcast.15, bf16[128,128]{1,0:T(8,128)(2,1)} %bitcast.16, bf16[128,128]{1,0:T(8,128)(2,1)} %bitcast.17, ...), custom_call_target="tpu_custom_call" | custom-call | tf_op jit(solution)/shard_map/layer_backward/pallas_call | solution.py:730
  101.4 2.4 %place_outputs.1 = (bf16[128,1024]{1,0:T(8,128)(2,1)}, bf16[128,128]{1,0:T(8,128)(2,1)}, bf16[128,128]{1,0:T(8,128)(2,1)}, bf16[10,128,384]{2,1,0:T(8,128)(2,1)}) custom-call(bf16[128,1024]{1,0:T(8,128)(2,1)} %get-tuple-element.12.refs_0_, bf16[128,128]{1,0:T(8,128)(2,1)} %get-tuple-element.13.refs_1_, bf16[128,128]{1,0:T(8,128)(2,1)} %get-tuple-element.14.refs_2_, ...), custom_call_target="tpu_custom_call" | custom-call | tf_op jit(solution)/shard_map/place_outputs/pallas_call | solution.py:741

commit v4 on v3

--- a/solution.py
+++ b/solution.py
@@ -75,9 +75,9 @@
 def kernel(
     q_ref, do_ref, k_ref, v_ref, mg_ref, ids_ref, comb_ref, w_ref,
     dq_ref, dk_ref, dv_ref, hid_ref,
-    kv, rows, picks, snd, rcv, sums, qs, dos, stat, dqt, dkv, xs1, xr1, xs2, xr2, zs, zr,
+    kv, rows, picks, snd, rcv, sums, qs, dos, stat, dqt, dkv, xs1, xr1, xs2, xr2, zs, za, zb, zr,
     ring_s, ring_r, kz_s, kz_r, xf_s, xf_r, xh_s, xh_r, xb_s, xb_r, xt_s, xt_r,
-    a2a_s, a2a_r, all_s, all_r, core_s, core_r, r1_s, r1_r, r2_s, r2_r, rz_s, rz_r,
+    a2a_s, a2a_r, all_s, all_r, core_s, core_r, r1_s, r1_r, r2_s, r2_r, za_s, za_r, rz_s, rz_r,
 ):
     y = lax.axis_index("dp")
     c = lax.axis_index("ctx")
@@ -121,15 +121,6 @@
 
     kv[c, :, :HEAD_DIM] = k_ref[...]
     kv[c, :, HEAD_DIM:] = v_ref[...]
-    rows[8, pl.ds(SIDE, TOK), :] = mg_ref[...]
-    rows[8, pl.ds(0, SIDE), :] = token_targets(
-        ids_ref[...].astype(F32), comb_ref[...].astype(F32)
-    )
-    for h in range(GROUP):
-        qs[pl.ds(h * TOK, TOK), :] = q_ref[:, h * HEAD_DIM : (h + 1) * HEAD_DIM]
-        dos[pl.ds(h * TOK, TOK), :] = do_ref[:, h * HEAD_DIM : (h + 1) * HEAD_DIM]
-    stat[0:1, :] = jnp.full((1, ROWS), MASKED, F32)
-    stat[1:3, :] = jnp.zeros((2, ROWS), F32)
     pl.semaphore_wait(barrier, 3 + 15 + 7)
 
     half = (pl.ds(0, TOK // 2), pl.ds(TOK // 2, TOK // 2))
@@ -315,13 +306,22 @@
         kz_copy(1, 0, zl).start()
 
     x_send(zl)
+    rows[8, pl.ds(SIDE, TOK), :] = mg_ref[...]
+    rows[8, pl.ds(0, SIDE), :] = token_targets(
+        ids_ref[...].astype(F32), comb_ref[...].astype(F32)
+    )
+    for h in range(GROUP):
+        qs[pl.ds(h * TOK, TOK), :] = q_ref[:, h * HEAD_DIM : (h + 1) * HEAD_DIM]
+        dos[pl.ds(h * TOK, TOK), :] = do_ref[:, h * HEAD_DIM : (h + 1) * HEAD_DIM]
+    stat[0:1, :] = jnp.full((1, ROWS), MASKED, F32)
+    stat[1:3, :] = jnp.zeros((2, ROWS), F32)
     ring(0, 0, 0, "start")
     ring(1, 1, 0, "start")
     ring(0, 1, 0, "start")
     ring(1, 0, 0, "start")
     stats(c, 1, 0)
 
-    @pl.loop(0, NL + 1)
+    @pl.loop(0, NL)
     def _(s):
         below, above = zl - 1 - s, zl + 1 + s
 
@@ -356,7 +356,7 @@
         for way, part in ((0, 0), (1, 1), (0, 1), (1, 0)):
             most = NL if way == part else NL - 1
 
-            @pl.when((s >= 1) & (s <= most))
+            @pl.when(s >= 1)
             def _():
                 ring(way, part, s - 1, "wait_recv")
 
@@ -373,7 +373,7 @@
             x_pass(zl - s)
             x_pass(zl + s)
 
-        @pl.when((s >= 2) & (s < NL))
+        @pl.when(s >= 2)
         def _():
             pack_rows((s - 2) // 2, s % 2)
 
@@ -387,6 +387,9 @@
 
     @pl.when(x == 0)
     def _():
+        ring(0, 0, NL - 1, "wait_recv")
+        ring(1, 1, NL - 1, "wait_recv")
+
         @pl.loop(0, 2)
         def _(n):
             pack_rows(3, n)
@@ -433,22 +436,42 @@
             ref, xr2.at[way, part], (r2_s.at[way, part], r2_r.at[way, part]), (x_up, x_down)[way]
         )
 
-    def rz_send(part, j):
+    side, mine = zl % 2, zl // 2
+
+    def block_rows(j):
+        return pl.ds(pl.multiple_of(j * SLICE, SLICE), SLICE)
+
+    def pair_copy(part):
+        sems = (za_s.at[part], za_r.at[part])
+        return remote(zs.at[part], za.at[part], sems, line_dev(zl + 1 - 2 * side))
+
+    def rz_send(part, n):
         return remote(
-            zs.at[part, j], zr.at[part, zl], (rz_s.at[part, j], rz_r.at[part, zl]), line_dev(j)
+            zb.at[part, n], zr.at[part, mine], (rz_s.at[part, n], rz_r.at[part, mine]),
+            line_dev(2 * n + side),
         )
 
-    def rz_got(part, j):
+    def rz_got(part, n):
         return remote(
-            zs.at[part, j], zr.at[part, j], (rz_s.at[part, j], rz_r.at[part, j]), line_dev(j)
+            zb.at[part, n], zr.at[part, n], (rz_s.at[part, n], rz_r.at[part, n]),
+            line_dev(2 * n + side),
         )
 
     def z_spread(part):
-        zs[part] = dkv[x, part].astype(BF16).reshape(NL, SLICE, WIDE)
-
-        @pl.loop(1, NL)
+        for n in range(4):
+            zs[part, n] = dkv[x, part, block_rows(2 * n + 1 - side), :].astype(BF16)
+        pair_copy(part).start()
+
+    def z_relay(part):
+        pair_copy(part).wait_recv()
+        for n in range(4):
+            total = dkv[x, part, block_rows(2 * n + side), :] + za[part, n].astype(F32)
+            dkv[x, part, block_rows(2 * n + side), :] = total
+            zb[part, n] = total.astype(BF16)
+
+        @pl.loop(1, 4)
         def _(i):
-            rz_send(part, (zl + i) % NL).start()
+            rz_send(part, (mine + i) % 4).start()
 
     @pl.when(x >= 2)
     def _():
@@ -495,6 +518,9 @@
 
     @pl.when(x >= 1)
     def _():
+        ring(0, 0, NL - 1, "wait_recv")
+        ring(1, 1, NL - 1, "wait_recv")
+
         @pl.loop(0, 2)
         def _(n):
             pack_rows(3, n)
@@ -553,7 +579,7 @@
 
     pl.loop(0, 3)(swap_rows)
 
-    @pl.loop(0, 4)
+    @pl.loop(0, PARTS)
     def _(part):
         @pl.when(x <= 2)
         def _():
@@ -567,11 +593,12 @@
 
             z_spread(part)
 
-    @pl.loop(1, 3)
-    def _(w):
-        all_copy(1 - core, w).wait_recv()
-
-    expert_group(1)
+        @pl.when((part >= 2) | ((x == 3) & (part >= 1)))
+        def _():
+            z_relay(jnp.where(x == 3, part - 1, part - 2))
+
+    pl.when(x <= 2)(lambda: z_relay(PARTS - 2))
+    pl.when(x >= 1)(lambda: z_relay(PARTS - 1))
     core_copy(core, plane).start()
 
     @pl.loop(1, 16)
@@ -579,6 +606,14 @@
         d = (plane + 16 - i) % 16
         a2a_in(3, d).wait_recv()
         core_copy(core, d).start()
+
+    pl.when(x == 0)(lambda: z_relay(PARTS - 1))
+
+    @pl.loop(1, 3)
+    def _(w):
+        all_copy(1 - core, w).wait_recv()
+
+    expert_group(1)
 
     @pl.loop(0, 16)
     def _(i):
@@ -608,11 +643,11 @@
 
     @pl.loop(0, PARTS)
     def _(part):
-        own = dkv[x, part, pl.ds(pl.multiple_of(zl * SLICE, SLICE), SLICE), :]
-        for i in range(1, NL):
-            j = (zl + i) % NL
-            rz_got(part, j).wait_recv()
-            own += zr[part, j].astype(F32)
+        own = dkv[x, part, block_rows(zl), :]
+        for i in range(1, 4):
+            n = (mine + i) % 4
+            rz_got(part, n).wait_recv()
+            own += zr[part, n].astype(F32)
         here = pl.ds(pl.multiple_of(part * SLICE, SLICE), SLICE)
         dk_ref[here, :] = (own[:, :HEAD_DIM] * SCALE).astype(BF16)
         dv_ref[here, :] = own[:, HEAD_DIM:].astype(BF16)
@@ -682,10 +717,13 @@
         def _():
             r2_copy(0, part).wait_send()
 
-    @pl.loop(1, NL)
-    def _(i):
-        for part in range(PARTS):
-            rz_send(part, (zl + i) % NL).wait_send()
+    @pl.loop(0, PARTS)
+    def _(part):
+        pair_copy(part).wait_send()
+
+        @pl.loop(1, 4)
+        def _(i):
+            rz_send(part, (mine + i) % 4).wait_send()
 
 
 def place(*refs):
@@ -719,12 +757,14 @@
         pltpu.VMEM((4, CHUNK, WIDE), BF16),
         pltpu.VMEM((2, 4, CHUNK, WIDE), BF16),
         pltpu.VMEM((2, 4, CHUNK, WIDE), BF16),
-        pltpu.VMEM((PARTS, NL, SLICE, WIDE), BF16),
-        pltpu.VMEM((PARTS, NL, SLICE, WIDE), BF16),
+        pltpu.VMEM((PARTS, 4, SLICE, WIDE), BF16),
+        pltpu.VMEM((PARTS, 4, SLICE, WIDE), BF16),
+        pltpu.VMEM((PARTS, 4, SLICE, WIDE), BF16),
+        pltpu.VMEM((PARTS, 4, SLICE, WIDE), BF16),
     ]
     for shape in (
         (2, 2, NL), (2, NL), (NL,), (NL,), (2, NL), (NL,),
-        (4, 16), (3,), (16,), (4,), (2, 4), (PARTS, NL),
+        (4, 16), (3,), (16,), (4,), (2, 4), (PARTS,), (PARTS, 4),
     ):
         scratch += [dma(shape), dma(shape)]
     dq, dk, dv, hidden = pl.pallas_call(

time: 104 us -> 102 us (0.981)
  Pallas kernels: 103 us -> 101 us
    pallas_call x1, Pallas kernels: 101 us -> 98.9 us  [per_device(): pl.pallas_call(kernel, out_shape=shapes, in_specs=[vmem] * 8, out_specs=(...]
where the time goes in v4:
time: 102 us
  Pallas kernels  101 us (99%)
    pallas_call x1, Pallas kernels, per_device(): pl.pallas_call(kernel, out_shape=shapes, in_specs=[vmem] * 8, out_specs=(...  98.9 us
    pallas_call x1, Pallas kernels, per_device(): pl.pallas_call(place, out_shape=shapes, in_specs=[vmem] * 4, out_specs=(v...  2.39 us

profile of v4, /device:TPU:8, one launch (start us, length us, event | category | flops | bytes accessed | tf_op | source)
XLA Modules:
  0.0 102.0 jit_solution(7499269588266741526)
XLA Ops:
  0.6 98.9 %layer_backward.1 = (bf16[128,1024]{1,0:T(8,128)(2,1)}, bf16[128,128]{1,0:T(8,128)(2,1)}, bf16[128,128]{1,0:T(8,128)(2,1)}, bf16[10,128,384]{2,1,0:T(8,128)(2,1)}) custom-call(bf16[128,1024]{1,0:T(8,128)(2,1)} %bitcast.14, bf16[128,1024]{1,0:T(8,128)(2,1)} %bitcast.15, bf16[128,128]{1,0:T(8,128)(2,1)} %bitcast.16, bf16[128,128]{1,0:T(8,128)(2,1)} %bitcast.17, ...), custom_call_target="tpu_custom_call" | custom-call | tf_op jit(solution)/shard_map/layer_backward/pallas_call | solution.py:770
  99.6 2.4 %place_outputs.1 = (bf16[128,1024]{1,0:T(8,128)(2,1)}, bf16[128,128]{1,0:T(8,128)(2,1)}, bf16[128,128]{1,0:T(8,128)(2,1)}, bf16[10,128,384]{2,1,0:T(8,128)(2,1)}) custom-call(bf16[128,1024]{1,0:T(8,128)(2,1)} %get-tuple-element.12.refs_0_, bf16[128,128]{1,0:T(8,128)(2,1)} %get-tuple-element.13.refs_1_, bf16[128,128]{1,0:T(8,128)(2,1)} %get-tuple-element.14.refs_2_, ...), custom_call_target="tpu_custom_call" | custom-call | tf_op jit(solution)/shard_map/place_outputs/pallas_call | solution.py:781

commit v5 on v4

--- a/solution.py
+++ b/solution.py
@@ -641,6 +641,71 @@
             here = pl.ds(pl.multiple_of(i * 4 * NL, 4 * NL), 4 * NL)
             hid_ref[n, here, :] = jnp.concatenate(parts, axis=0).astype(BF16)
 
+    @pl.loop(0, NL)
+    def _(s):
+        @pl.when((zl < NL - 1) & (zl - s >= 0))
+        def _():
+            kz_copy(0, s, zl - s).wait_send()
+
+        @pl.when((zl > 0) & (zl + s < NL))
+        def _():
+            kz_copy(1, s, zl + s).wait_send()
+
+        ring(0, 0, s, "wait_send")
+        ring(1, 1, s, "wait_send")
+
+        @pl.when(s < NL - 1)
+        def _():
+            ring(0, 1, s, "wait_send")
+            ring(1, 0, s, "wait_send")
+
+        @pl.when(x <= 2)
+        def _():
+            xf_copy(x, s).wait_send()
+
+        @pl.when(x == 0)
+        def _():
+            xb_copy(0, x, s).wait_send()
+
+        @pl.when(x <= 1)
+        def _():
+            xb_copy(1, x, s).wait_send()
+
+        @pl.when((x == 1) | (x == 2))
+        def _():
+            xh_copy(x - 1, s).wait_send()
+
+        @pl.when((x == 3) | (x == 0))
+        def _():
+            xt_copy((x + 1) % NX, s).wait_send()
+
+    @pl.loop(0, 3)
+    def _(w):
+        all_copy(core, w).wait_send()
+
+    core_copy(core, plane).wait_send()
+
+    @pl.loop(0, 15)
+    def _(r):
+        for w in range(4):
+            a2a_out(w, r).wait_send()
+        core_copy(core, (plane + r + 1) % 16).wait_send()
+
+    @pl.loop(0, 4)
+    def _(part):
+        @pl.when(x >= 2)
+        def _():
+            pl.when(part < 2)(lambda: r1_copy(0, part).wait_send())
+            pl.when(part >= 2)(lambda: r1_copy(1, part).wait_send())
+
+        @pl.when(x >= 1)
+        def _():
+            r2_copy(1, part).wait_send()
+
+        @pl.when((x == 3) | ((x == 0) & (part < 2)))
+        def _():
+            r2_copy(0, part).wait_send()
+
     @pl.loop(0, PARTS)
     def _(part):
         own = dkv[x, part, block_rows(zl), :]
@@ -651,71 +716,6 @@
         here = pl.ds(pl.multiple_of(part * SLICE, SLICE), SLICE)
         dk_ref[here, :] = (own[:, :HEAD_DIM] * SCALE).astype(BF16)
         dv_ref[here, :] = own[:, HEAD_DIM:].astype(BF16)
-
-    @pl.loop(0, NL)
-    def _(s):
-        @pl.when((zl < NL - 1) & (zl - s >= 0))
-        def _():
-            kz_copy(0, s, zl - s).wait_send()
-
-        @pl.when((zl > 0) & (zl + s < NL))
-        def _():
-            kz_copy(1, s, zl + s).wait_send()
-
-        ring(0, 0, s, "wait_send")
-        ring(1, 1, s, "wait_send")
-
-        @pl.when(s < NL - 1)
-        def _():
-            ring(0, 1, s, "wait_send")
-            ring(1, 0, s, "wait_send")
-
-        @pl.when(x <= 2)
-        def _():
-            xf_copy(x, s).wait_send()
-
-        @pl.when(x == 0)
-        def _():
-            xb_copy(0, x, s).wait_send()
-
-        @pl.when(x <= 1)
-        def _():
-            xb_copy(1, x, s).wait_send()
-
-        @pl.when((x == 1) | (x == 2))
-        def _():
-            xh_copy(x - 1, s).wait_send()
-
-        @pl.when((x == 3) | (x == 0))
-        def _():
-            xt_copy((x + 1) % NX, s).wait_send()
-
-    @pl.loop(0, 3)
-    def _(w):
-        all_copy(core, w).wait_send()
-
-    core_copy(core, plane).wait_send()
-
-    @pl.loop(0, 15)
-    def _(r):
-        for w in range(4):
-            a2a_out(w, r).wait_send()
-        core_copy(core, (plane + r + 1) % 16).wait_send()
-
-    @pl.loop(0, 4)
-    def _(part):
-        @pl.when(x >= 2)
-        def _():
-            pl.when(part < 2)(lambda: r1_copy(0, part).wait_send())
-            pl.when(part >= 2)(lambda: r1_copy(1, part).wait_send())
-
-        @pl.when(x >= 1)
-        def _():
-            r2_copy(1, part).wait_send()
-
-        @pl.when((x == 3) | ((x == 0) & (part < 2)))
-        def _():
-            r2_copy(0, part).wait_send()
 
     @pl.loop(0, PARTS)
     def _(part):

time: 102 us -> 102 us (level)
  no operation moved by 1% of the time
where the time goes in v5:
time: 102 us; the launch traced here: 101 us
  Pallas kernels  101 us (99%)
    pallas_call x1, Pallas kernels, per_device(): pl.pallas_call(kernel, out_shape=shapes, in_specs=[vmem] * 8, out_specs=(...  98.3 us
    pallas_call x1, Pallas kernels, per_device(): pl.pallas_call(place, out_shape=shapes, in_specs=[vmem] * 4, out_specs=(v...  2.39 us

profile of v5, /device:TPU:8, one launch (start us, length us, event | category | flops | bytes accessed | tf_op | source)
XLA Modules:
  0.0 101.4 jit_solution(2537870038749866287)
XLA Ops:
  0.6 98.3 %layer_backward.1 = (bf16[128,1024]{1,0:T(8,128)(2,1)}, bf16[128,128]{1,0:T(8,128)(2,1)}, bf16[128,128]{1,0:T(8,128)(2,1)}, bf16[10,128,384]{2,1,0:T(8,128)(2,1)}) custom-call(bf16[128,1024]{1,0:T(8,128)(2,1)} %bitcast.14, bf16[128,1024]{1,0:T(8,128)(2,1)} %bitcast.15, bf16[128,128]{1,0:T(8,128)(2,1)} %bitcast.16, bf16[128,128]{1,0:T(8,128)(2,1)} %bitcast.17, ...), custom_call_target="tpu_custom_call" | custom-call | tf_op jit(solution)/shard_map/layer_backward/pallas_call | solution.py:770
  99.0 2.4 %place_outputs.1 = (bf16[128,1024]{1,0:T(8,128)(2,1)}, bf16[128,128]{1,0:T(8,128)(2,1)}, bf16[128,128]{1,0:T(8,128)(2,1)}, bf16[10,128,384]{2,1,0:T(8,128)(2,1)}) custom-call(bf16[128,1024]{1,0:T(8,128)(2,1)} %get-tuple-element.12.refs_0_, bf16[128,128]{1,0:T(8,128)(2,1)} %get-tuple-element.13.refs_1_, bf16[128,128]{1,0:T(8,128)(2,1)} %get-tuple-element.14.refs_2_, ...), custom_call_target="tpu_custom_call" | custom-call | tf_op jit(solution)/shard_map/place_outputs/pallas_call | solution.py:781
